TPU v7x, 1024 devices: a whole 4x8x16 slice. The times are simulated.
1024 devices in a mesh: row: 16 (over x_hi, y), col: 64 (over x_lo, z, core).
Axes of the slice: x: 4 (x_hi: 2, x_lo: 2; x = x_hi * 2 + x_lo), y: 8, z: 16, core: 2. Of those that a mesh axis runs over, the one named last changes fastest.
Arguments:
- vectors: bfloat16 [8, 262144], P(None, ('row', 'col')), may hold values from -6 to 6
- matrix_tiles: bfloat16 [32768, 128, 128], P(('row', 'col')), may hold values from -0.1875 to 0.1875
- tile_row: int32 [32768], P(('row', 'col')), may hold values from 0 to 127, as said below
- tile_col: int32 [32768], P(('row', 'col')), may hold values from 0 to 31, as said below
Outputs:
- applied: float32 [8, 262144], P(None, ('row', 'col'))
Inputs may be any that keep to these rules, and one draw needn't show every extreme that they name: `tile_row`: global tile row >= global tile column for every stored tile; tiles may repeat. tile_col // 2 never exceeds the device's index along row.
All inputs are finite; a program needn't handle non-finite values.
Results may differ from a plain program's by a relative error of at most 0.0003.
Values may be sent and summed in bfloat16 or wider, within the bound.
No kernel may reach another device: no remote copies, remote signals or barrier semaphores. Data moves between devices by JAX's collectives and lax.ppermute only.
A program may use at most 32 MiB of HBM per device.

v0:
```python
import jax
import jax.numpy as jnp
from jax import lax
from jax.sharding import PartitionSpec as P


def per_device(vectors, matrix_tiles, tile_row, tile_col):
    count_vec = vectors.shape[0]
    seg_len = vectors.shape[1]
    tile_width = matrix_tiles.shape[1]
    gathered_col = lax.all_gather(vectors, "row", axis=1, tiled=True)
    gathered_row = lax.all_gather(vectors, "col", axis=1, tiled=True)
    col_blocks = gathered_col.reshape(count_vec, -1, tile_width)
    row_blocks = gathered_row.reshape(count_vec, -1, tile_width)
    picked_col = jnp.take(col_blocks, tile_col, axis=1)
    picked_row = jnp.take(row_blocks, tile_row, axis=1)
    row_terms = jnp.einsum(
        "ktj,tij->tki", picked_col, matrix_tiles, preferred_element_type=jnp.float32
    )
    col_terms = jnp.einsum(
        "kti,tij->ktj", picked_row, matrix_tiles, preferred_element_type=jnp.float32
    )
    col_part = jnp.zeros((count_vec, col_blocks.shape[1], tile_width), jnp.float32)
    col_part = col_part.at[:, tile_col].add(col_terms).reshape(count_vec, -1)
    col_sum = lax.psum_scatter(col_part, "row", scatter_dimension=1, tiled=True)
    total_rows = row_blocks.shape[1]
    row_part = jnp.zeros((total_rows, count_vec, tile_width), jnp.float32)
    row_part = row_part.at[tile_row].add(row_terms)
    row_sum = lax.psum_scatter(row_part, "col", scatter_dimension=0, tiled=True)
    return row_sum.transpose(1, 0, 2).reshape(count_vec, seg_len) + col_sum


def solution(mesh):
    in_specs = (
        P(None, ("row", "col")),
        P(("row", "col"), None, None),
        P(("row", "col")),
        P(("row", "col")),
    )
    out_specs = P(None, ("row", "col"))
    return jax.shard_map(
        per_device, mesh=mesh, in_specs=in_specs, out_specs=out_specs, check_vma=False
    )
```

profile of v0, /device:TPU:1, one launch (start us, length us, event | category | flops | bytes accessed | tf_op | source)
XLA Modules:
  0.0 532.8 jit_solution(10669664551470771572)
XLA Ops:
  6.5 0.0 copy-start
  6.5 0.0 copy-start.4
  6.5 0.0 reduce-scatter.5.cloned.1.call-start
  6.5 0.0 copy-start.5
  6.5 0.7 compare_select_fusion.1
  7.3 0.0 copy-done.4
  7.3 0.0 copy-start.3
  7.3 0.0 copy-done.5
  7.3 0.6 copy-done.3
  8.0 78.5 %all_gather.7 = bf16[8,16384]{1,0:T(8,128)(2,1)S(1)} all-gather(bf16[8,256]{1,0:T(8,128)(2,1)S(1)} %copy-done.3), channel_id=1, replica_groups=mesh['row'=16,'col'=64] {'col'}, dimensions={1}, use_global_device_ids=true | all-gather | bytes 266240 | tf_op jit(solution)/shard_map/all_gather | solution.py:12
  86.5 0.6 gather_fusion.1
  87.0 0.0 copy-done
  87.1 0.4 fusion
  87.5 1.7 scatter_fusion.1
  89.2 0.0 copy-start.2
  89.2 0.6 copy-done.2
  89.9 0.0 reduce-scatter.5.cloned.1.call-update
  89.9 0.0 reduce-scatter.3.cloned.1.call-start
  90.0 34.5 %all_gather.6 = bf16[8,4096]{1,0:T(8,128)(2,1)S(1)} all-gather(bf16[8,256]{1,0:T(8,128)(2,1)S(1)} %copy-done.3), channel_id=1, replica_groups=mesh['row'=16,'col'=64] {'row'}, dimensions={1}, use_global_device_ids=true | all-gather | bytes 69632 | tf_op jit(solution)/shard_map/all_gather | solution.py:11
  124.5 0.6 gather_fusion
  125.1 0.7 fusion.2
  125.8 0.1 broadcast_in_dim.30
  125.8 1.6 scatter_fusion
  127.5 0.0 copy-start.1
  127.5 0.8 copy-done.1
  128.3 0.0 reduce-scatter.3.cloned.1.call-update
  128.3 162.6 %reduce-scatter.5.cloned.1.call-done = f32[8,256]{1,0:T(8,128)} async-done(((f32[8,4096]{1,0:T(8,128)}), f32[8,256]{1,0:T(8,128)}) %reduce-scatter.5.cloned.1.call-update) | async-done | bytes 8208 | tf_op jit(solution)/shard_map/reduce_scatter | solution.py:25
  290.9 233.7 %reduce-scatter.3.cloned.1.call-done = f32[2,8,128]{2,1,0:T(8,128)} async-done(((f32[128,8,128]{2,1,0:T(8,128)}), f32[2,8,128]{2,1,0:T(8,128)}) %reduce-scatter.3.cloned.1.call-update) | async-done | bytes 8208 | tf_op jit(solution)/shard_map/reduce_scatter | solution.py:29
  524.6 1.3 bitcast_add_fusion
  (6 shorter events, 0.1 us)
Async XLA Ops:
  6.5 80.5 %copy-start = (bf16[32,128,128]{2,1,0:T(8,128)(2,1)S(1)}, bf16[32,128,128]{2,1,0:T(8,128)(2,1)}, u32[]{:S(2)}) copy-start(bf16[32,128,128]{2,1,0:T(8,128)(2,1)} %param.5) | copy-start | bytes 3145732
  6.5 0.8 copy-start.4
  6.5 284.3 %reduce-scatter.5.cloned.1.call-start = ((), (), s32[]{:S(2)}) async-start(), calls=%async_computation.3 | async-start | bytes 139264 | tf_op jit(solution)/shard_map/reduce_scatter | solution.py:25
  6.5 0.8 copy-start.5
  7.3 0.7 copy-start.3
  89.2 0.7 copy-start.2
  89.9 434.7 %reduce-scatter.3.cloned.1.call-start = ((), (), s32[]{:S(2)}) async-start(), calls=%async_computation.2 | async-start | bytes 532480 | tf_op jit(solution)/shard_map/reduce_scatter | solution.py:29
  127.5 0.8 copy-start.1
Sparse Core Ops, SparseCore 0:
  90.0 200.7 reduce-scatter.4
  294.6 229.9 reduce-scatter.2
where the time goes:
time: 536 us; the launch traced here: 533 us
  waiting for transfers between devices  396 us (74%)
  blocking collectives  113 us (21%)
  between operations  13.5 us (3%)
  other arithmetic  5.43 us (1%)
    reduce_scatter x1, waiting for transfers between devices, per_device(): row_sum = lax.psum_scatter(row_part, 'col', scatter_dimension=0, tiled=True)  234 us
    reduce_scatter x1, waiting for transfers between devices, per_device(): col_sum = lax.psum_scatter(col_part, 'row', scatter_dimension=1, tiled=True)  163 us
    all_gather x1, blocking collectives, per_device(): gathered_row = lax.all_gather(vectors, 'col', axis=1, tiled=True)  78.5 us
    all_gather x1, blocking collectives, per_device(): gathered_col = lax.all_gather(vectors, 'row', axis=1, tiled=True)  34.5 us
  transfers between devices with their start and end apart: 2, of which 2 were waited for; matrix products, arithmetic and copies ran while one was open for 1% of the time, Pallas kernels for 0%

commit v1 on v0

v1 whole, which is shorter than its diff:
```python
import jax
import jax.numpy as jnp
from jax import lax
from jax.experimental import pallas as pl
from jax.experimental.pallas import tpu as pltpu
from jax.sharding import Mesh, PartitionSpec as P

AXES = ("xh", "y", "xl", "z", "core")
SIZES = (2, 8, 2, 16, 2)
TPD, K, TILE = 32, 8, 128
VM = pl.BlockSpec(memory_space=pltpu.VMEM)
SM = pl.BlockSpec(memory_space=pltpu.SMEM)


def half_of(block, half):
    return jnp.where(half == 1, block[:, TILE:], block[:, :TILE])


def row_kernel(tr, tc, seg, tiles, keep, send):
    core = lax.axis_index("core")
    keep[...] = jnp.zeros_like(keep)
    send[...] = jnp.zeros_like(send)
    for t in range(TPD):
        r, c = tr[t], tc[t]
        x = half_of(seg[c // 2], c % 2)
        y = lax.dot_general(x, tiles[t], (((1,), (1,)), ((), ())), preferred_element_type=jnp.float32)
        mine = ((r // 2) % 2) == core
        at = (r // 4) * 2 + r % 2
        keep[at] += jnp.where(mine, y, 0.0)
        send[at] += jnp.where(mine, 0.0, y)


def col_kernel(tr, tc, seg, tiles, keep, send):
    xh = lax.axis_index("xh")
    keep[...] = jnp.zeros_like(keep)
    send[...] = jnp.zeros_like(send)
    for t in range(TPD):
        r, c = tr[t], tc[t]
        q = r // 2
        x = half_of(seg[q % 2, (q // 2) % 16, q // 32], r % 2)
        y = jnp.dot(x, tiles[t], preferred_element_type=jnp.float32)
        s = c // 2
        mine = (s // 8) == xh
        at = (s % 8) * 2 + c % 2
        keep[at] += jnp.where(mine, y, 0.0)
        send[at] += jnp.where(mine, 0.0, y)


def products(kernel, owners, tr, tc, seg, tiles):
    part = jax.ShapeDtypeStruct((owners, K, TILE), jnp.float32)
    return pl.pallas_call(
        kernel,
        out_shape=(part, part),
        in_specs=[SM, SM, VM, VM],
        out_specs=(VM, VM),
        cost_estimate=pl.CostEstimate(flops=2 * TPD * K * TILE * TILE, bytes_accessed=2 << 20, transcendentals=0),
        compiler_params=pltpu.CompilerParams(vmem_limit_bytes=16 << 20),
    )(tr, tc, seg, tiles)


def total_kernel(a, b, out):
    out[:, :TILE] = jnp.sum(a[:, 0], axis=0) + jnp.sum(b[:, 0], axis=0)
    out[:, TILE:] = jnp.sum(a[:, 1], axis=0) + jnp.sum(b[:, 1], axis=0)


def swap(n):
    return [(i, n - 1 - i) for i in range(n)]


def per_device(v, tiles, tr, tc):
    seg_row = lax.all_to_all(jnp.broadcast_to(v[None], (16, K, 256)), ("xh", "y"), 0, 0, tiled=True)
    pair = lax.all_gather(v, "xl", axis=0)
    seg_row, pair = lax.optimization_barrier((seg_row, pair))
    spread = jnp.broadcast_to(pair[None], (16, 2, K, 256))
    seg_z = lax.all_to_all(spread, "z", 0, 0, tiled=True)
    keep, send = products(row_kernel, 64, tr, tc, seg_row, tiles)
    other = lax.all_gather(send, "core", axis=0)
    core = lax.axis_index("core")
    row_part = keep + lax.dynamic_index_in_dim(other, 1 - core, 0, keepdims=False)
    row_part, seg_z = lax.optimization_barrier((row_part, seg_z))
    row_got = lax.all_to_all(row_part.reshape(32, 2, K, TILE), ("xl", "z"), 0, 0, tiled=True)
    seg_col = lax.all_gather(seg_z, "core", axis=0)
    keep, send = products(col_kernel, 16, tr, tc, seg_col, tiles)
    col_part = keep + lax.ppermute(send, "xh", swap(2))
    col_part, row_got = lax.optimization_barrier((col_part, row_got))
    col_got = lax.all_to_all(col_part.reshape(8, 2, K, TILE), "y", 0, 0, tiled=True)
    return pl.pallas_call(
        total_kernel,
        out_shape=jax.ShapeDtypeStruct((K, 256), jnp.float32),
        in_specs=[VM, VM],
        out_specs=VM,
    )(row_got, col_got)


def solution(mesh):
    fine = Mesh(mesh.devices.reshape(SIZES), AXES)
    return jax.shard_map(
        per_device,
        mesh=fine,
        in_specs=(P(None, AXES), P(AXES, None, None), P(AXES), P(AXES)),
        out_specs=P(None, AXES),
        check_vma=False,
    )
```

time: 536 us -> 94.1 us (0.18)
  waiting for transfers between devices: 396 us -> 23.2 us
  blocking collectives: 113 us -> 20 us
  starting transfers between devices: 0.04 us -> 39.9 us
  between operations: 13.5 us -> 0.08 us
    reduce_scatter x2 -> x0, waiting for transfers between devices: 396 us -> none  [the longest x1 234 us: per_device(): row_sum = lax.psum_scatter(row_part, 'col', scatter_dimension=0, tiled=True)]
    all_gather x2 -> x3, blocking collectives: 113 us -> 9.66 us  [the longest x1 4.18 us: per_device(): other = lax.all_gather(send, 'core', axis=0)]
    all_to_all x0 -> x3, starting transfers between devices: none -> 37 us  [the longest x1 18.6 us: per_device(): seg_z = lax.all_to_all(spread, 'z', 0, 0, tiled=True)]
    all_to_all x0 -> x3, waiting for transfers between devices: none -> 18.2 us  [the longest x1 8.57 us: per_device(): lax.all_to_all(row_part.reshape(32, 2, K, TILE), ('xl', 'z'), 0, 0, tiled...]
    all_to_all x0 -> x1, blocking collectives: none -> 10.4 us  [per_device(): lax.all_to_all(col_part.reshape(8, 2, K, TILE), 'y', 0, 0, tiled=True)]
  transfers between devices with their start and end apart: 2 -> 4, of which waited for: 2 -> 4; matrix products, arithmetic and copies ran while one was open for 1% -> 1% of each run, Pallas kernels for 0% -> 3%
where the time goes in v1:
time: 94.1 us; the launch traced here: 92.2 us
  starting transfers between devices  39.9 us (42%)
  waiting for transfers between devices  23.2 us (25%)
  blocking collectives  20 us (21%)
  Pallas kernels  4.34 us (5%)
  local copies, waits for them, and re-layouts  3.86 us (4%)
    all_to_all x1, starting transfers between devices, per_device(): seg_z = lax.all_to_all(spread, 'z', 0, 0, tiled=True)  18.6 us
    all_to_all x1, blocking collectives, per_device(): lax.all_to_all(col_part.reshape(8, 2, K, TILE), 'y', 0, 0, tiled=True)  10.4 us
    all_to_all x1, starting transfers between devices, per_device(): lax.all_to_all(jnp.broadcast_to(v[None], (16, K, 256)), ('xh', 'y'), 0, 0...  10.3 us
    all_to_all x1, waiting for transfers between devices, per_device(): lax.all_to_all(row_part.reshape(32, 2, K, TILE), ('xl', 'z'), 0, 0, tiled...  8.57 us
    all_to_all x1, starting transfers between devices, per_device(): lax.all_to_all(row_part.reshape(32, 2, K, TILE), ('xl', 'z'), 0, 0, tiled...  8.1 us
    all_to_all x1, waiting for transfers between devices, per_device(): lax.all_to_all(jnp.broadcast_to(v[None], (16, K, 256)), ('xh', 'y'), 0, 0...  5.68 us
    ppermute x1, waiting for transfers between devices, per_device(): col_part = keep + lax.ppermute(send, 'xh', swap(2))  5.05 us
    all_gather x1, blocking collectives, per_device(): other = lax.all_gather(send, 'core', axis=0)  4.18 us
  transfers between devices with their start and end apart: 4, of which 4 were waited for; matrix products, arithmetic and copies ran while one was open for 1% of the time, Pallas kernels for 3%

profile of v1, /device:TPU:1, one launch (start us, length us, event | category | flops | bytes accessed | tf_op | source)
XLA Modules:
  0.0 92.2 jit_solution(464018060297908988)
XLA Ops:
  0.0 1.3 %broadcast_in_dim.6 = bf16[16,8,256]{2,1,0:T(8,128)(2,1)} broadcast(bf16[8,256]{1,0:T(8,128)(2,1)} %param.4), dimensions={1,2} | broadcast | bytes 69632 | tf_op jit(solution)/shard_map/broadcast_in_dim | solution.py:71
  1.3 0.0 copy-start.5
  1.3 10.3 %all-to-all-start = ((bf16[16,8,256]{2,1,0:T(8,128)(2,1)}), bf16[16,8,256]{2,1,0:T(8,128)(2,1)S(1)}, u32[]{:S(2)}, u32[]{:S(2)}) async-start(bf16[16,8,256]{2,1,0:T(8,128)(2,1)} %broadcast_in_dim.6), calls=%async_computation | async-start | bytes 131072 | tf_op jit(solution)/shard_map/all_to_all | solution.py:71
  11.7 0.0 copy-done.5
  11.7 3.2 %all-gather = bf16[16,256]{1,0:T(8,128)(2,1)S(1)} all-gather(bf16[8,256]{1,0:T(8,128)(2,1)S(1)} %copy-done.5), channel_id=2, replica_groups=mesh['xh'=2,'y'=8,'xl'=2,'z'=16,'core'=2] {'xl'}, dimensions={0}, use_global_device_ids=true | all-gather | bytes 12288 | tf_op jit(solution)/shard_map/all_gather | solution.py:72
  14.9 5.7 %all-to-all-done.seg = bf16[16,8,256]{2,1,0:T(8,128)(2,1)S(1)} async-done(((bf16[16,8,256]{2,1,0:T(8,128)(2,1)}), bf16[16,8,256]{2,1,0:T(8,128)(2,1)S(1)}, u32[]{:S(2)}, u32[]{:S(2)}) %all-to-all-start) | async-done | bytes 65568 | tf_op jit(solution)/shard_map/all_to_all | solution.py:71
  20.5 0.7 broadcast_in_dim.16
  21.2 18.6 %all-to-all-start.1 = ((bf16[16,2,8,256]{3,2,1,0:T(8,128)(2,1)}), bf16[16,2,8,256]{3,2,1,0:T(8,128)(2,1)S(1)}, u32[]{:S(2)}, u32[]{:S(2)}) async-start(bf16[16,2,8,256]{3,2,1,0:T(8,128)(2,1)} %broadcast_in_dim.16), calls=%async_computation.1 | async-start | bytes 262144 | tf_op jit(solution)/shard_map/all_to_all | solution.py:75
  39.8 0.0 copy-start.2
  39.8 0.0 copy-start.3
  39.8 0.6 copy-done.2
  40.5 0.0 copy-done.3
  40.5 0.0 copy-start
  40.5 1.2 %copy-done = bf16[32,128,128]{2,1,0:T(8,128)(2,1)S(1)} copy-done((bf16[32,128,128]{2,1,0:T(8,128)(2,1)S(1)}, bf16[32,128,128]{2,1,0:T(8,128)(2,1)}, u32[]{:S(2)}) %copy-start) | copy-done | bytes 1048600
  41.7 1.2 %shard_map.46 = (f32[64,8,128]{2,1,0:T(8,128)S(1)}, f32[64,8,128]{2,1,0:T(8,128)S(1)}) custom-call(s32[32]{0:T(128)S(1)} %copy-done.2, s32[32]{0:T(128)S(1)} %copy-done.3, bf16[16,8,256]{2,1,0:T(8,128)(2,1)S(1)} %all-to-all-done.seg, bf16[32,128,128]{2,1,0:T(8,128)(2,1)S(1)} %copy-done), custom_call_target="tpu_custom_call" | custom-call | flops 8388608 | bytes 2097152 | tf_op jit(solution)/shard_map/pallas_call | solution.py:51
  42.9 4.2 %all-gather.1 = f32[128,8,128]{2,1,0:T(8,128)S(1)} all-gather(f32[64,8,128]{2,1,0:T(8,128)S(1)} %get-tuple-element.17), channel_id=3, replica_groups=mesh['xh'=2,'y'=8,'xl'=2,'z'=16,'core'=2] {'core'}, dimensions={0}, use_global_device_ids=true | all-gather | bytes 786432 | tf_op jit(solution)/shard_map/all_gather | solution.py:77
  47.1 0.0 copy-start.1
  47.1 0.7 bitcast_add_fusion
  47.9 4.0 %all-to-all-done.1 = bf16[16,2,8,256]{3,2,1,0:T(8,128)(2,1)S(1)} async-done(((bf16[16,2,8,256]{3,2,1,0:T(8,128)(2,1)}), bf16[16,2,8,256]{3,2,1,0:T(8,128)(2,1)S(1)}, u32[]{:S(2)}, u32[]{:S(2)}) %all-to-all-start.1) | async-done | bytes 131104 | tf_op jit(solution)/shard_map/all_to_all | solution.py:75
  51.8 8.1 %all-to-all-start.2 = ((f32[32,2,8,128]{3,2,1,0:T(8,128)}), f32[32,2,8,128]{3,2,1,0:T(8,128)S(1)}, u32[]{:S(2)}, u32[]{:S(2)}) async-start(f32[32,2,8,128]{3,2,1,0:T(8,128)} %bitcast.4), calls=%async_computation.2 | async-start | bytes 524288 | tf_op jit(solution)/shard_map/all_to_all | solution.py:81
  59.9 2.3 %all-gather.2 = bf16[32,2,8,256]{3,2,1,0:T(8,128)(2,1)S(1)} all-gather(bf16[16,2,8,256]{3,2,1,0:T(8,128)(2,1)S(1)} %all-to-all-done.1), channel_id=4, replica_groups=mesh['xh'=2,'y'=8,'xl'=2,'z'=16,'core'=2] {'core'}, dimensions={0}, use_global_device_ids=true | all-gather | bytes 393216 | tf_op jit(solution)/shard_map/all_gather | solution.py:82
  62.2 0.0 copy-done.1
  62.2 1.5 %shard_map.47 = (f32[16,8,128]{2,1,0:T(8,128)S(1)}, f32[16,8,128]{2,1,0:T(8,128)S(1)}) custom-call(s32[32]{0:T(128)S(1)} %copy-done.2, s32[32]{0:T(128)S(1)} %copy-done.3, bf16[2,16,2,8,256]{4,3,2,1,0:T(8,128)(2,1)S(1)} %bitcast.7, bf16[32,128,128]{2,1,0:T(8,128)(2,1)S(1)} %copy-done.1), custom_call_target="tpu_custom_call" | custom-call | flops 8388608 | bytes 2097152 | tf_op jit(solution)/shard_map/pallas_call | solution.py:51
  63.7 2.9 %collective-permute-start = (f32[16,8,128]{2,1,0:T(8,128)S(1)}, f32[16,8,128]{2,1,0:T(8,128)S(1)}, u32[]{:S(2)}, u32[]{:S(2)}) collective-permute-start(f32[16,8,128]{2,1,0:T(8,128)S(1)} %get-tuple-element.21), channel_id=1, source_target_pairs={{0,512},{512,0},{1,513},{513,1},{2,514},{514,2},{3,515},{515,3},{4... | collective-permute-start | bytes 196616 | tf_op jit(solution)/shard_map/ppermute | solution.py:84
  66.6 5.0 %collective-permute-done = f32[16,8,128]{2,1,0:T(8,128)S(1)} collective-permute-done((f32[16,8,128]{2,1,0:T(8,128)S(1)}, f32[16,8,128]{2,1,0:T(8,128)S(1)}, u32[]{:S(2)}, u32[]{:S(2)}) %collective-permute-start) | collective-permute-done | bytes 65568 | tf_op jit(solution)/shard_map/ppermute | solution.py:84
  71.7 8.6 %all-to-all-done.2.a = f32[32,2,8,128]{3,2,1,0:T(8,128)S(1)} async-done(((f32[32,2,8,128]{3,2,1,0:T(8,128)}), f32[32,2,8,128]{3,2,1,0:T(8,128)S(1)}, u32[]{:S(2)}, u32[]{:S(2)}) %all-to-all-start.2) | async-done | bytes 262176 | tf_op jit(solution)/shard_map/all_to_all | solution.py:81
  80.3 0.0 copy-start.4
  80.3 10.4 %all_to_all.20.b = f32[8,2,8,128]{3,2,1,0:T(8,128)} all-to-all(f32[8,2,8,128]{3,2,1,0:T(8,128)S(1)} %bitcast.9), channel_id=1, replica_groups=mesh['xh'=2,'y'=8,'xl'=2,'z'=16,'core'=2] {'y'}, dimensions={0} | all-to-all | bytes 131072 | tf_op jit(solution)/shard_map/all_to_all | solution.py:86
  90.7 0.0 copy-done.4
  90.7 1.6 %shard_map.48 = f32[8,256]{1,0:T(8,128)} custom-call(f32[32,2,8,128]{3,2,1,0:T(8,128)} %copy-done.4, f32[8,2,8,128]{3,2,1,0:T(8,128)} %all_to_all.20.b), custom_call_target="tpu_custom_call" | custom-call | tf_op jit(solution)/shard_map/pallas_call | solution.py:87
  (1 shorter events, 0.0 us)
Async XLA Ops:
  1.3 10.4 %copy-start.5 = (bf16[8,256]{1,0:T(8,128)(2,1)S(1)}, bf16[8,256]{1,0:T(8,128)(2,1)}, u32[]{:S(2)}) copy-start(bf16[8,256]{1,0:T(8,128)(2,1)} %param.4) | copy-start | bytes 12292
  1.3 19.2 %all-to-all-start = ((bf16[16,8,256]{2,1,0:T(8,128)(2,1)}), bf16[16,8,256]{2,1,0:T(8,128)(2,1)S(1)}, u32[]{:S(2)}, u32[]{:S(2)}) async-start(bf16[16,8,256]{2,1,0:T(8,128)(2,1)} %broadcast_in_dim.6), calls=%async_computation | async-start | bytes 131072 | tf_op jit(solution)/shard_map/all_to_all | solution.py:71
  21.2 30.6 %all-to-all-start.1 = ((bf16[16,2,8,256]{3,2,1,0:T(8,128)(2,1)}), bf16[16,2,8,256]{3,2,1,0:T(8,128)(2,1)S(1)}, u32[]{:S(2)}, u32[]{:S(2)}) async-start(bf16[16,2,8,256]{3,2,1,0:T(8,128)(2,1)} %broadcast_in_dim.16), calls=%async_computation.1 | async-start | bytes 262144 | tf_op jit(solution)/shard_map/all_to_all | solution.py:75
  39.8 0.7 copy-start.2
  39.8 0.7 copy-start.3
  40.5 1.2 %copy-start = (bf16[32,128,128]{2,1,0:T(8,128)(2,1)S(1)}, bf16[32,128,128]{2,1,0:T(8,128)(2,1)}, u32[]{:S(2)}) copy-start(bf16[32,128,128]{2,1,0:T(8,128)(2,1)} %tiles.3) | copy-start | bytes 3145732
  47.1 15.1 %copy-start.1 = (bf16[32,128,128]{2,1,0:T(8,128)(2,1)S(1)}, bf16[32,128,128]{2,1,0:T(8,128)(2,1)}, u32[]{:S(2)}) copy-start(bf16[32,128,128]{2,1,0:T(8,128)(2,1)} %tiles.3) | copy-start | bytes 3145732
  51.8 28.5 %all-to-all-start.2 = ((f32[32,2,8,128]{3,2,1,0:T(8,128)}), f32[32,2,8,128]{3,2,1,0:T(8,128)S(1)}, u32[]{:S(2)}, u32[]{:S(2)}) async-start(f32[32,2,8,128]{3,2,1,0:T(8,128)} %bitcast.4), calls=%async_computation.2 | async-start | bytes 524288 | tf_op jit(solution)/shard_map/all_to_all | solution.py:81
  63.7 8.0 %collective-permute-start = (f32[16,8,128]{2,1,0:T(8,128)S(1)}, f32[16,8,128]{2,1,0:T(8,128)S(1)}, u32[]{:S(2)}, u32[]{:S(2)}) collective-permute-start(f32[16,8,128]{2,1,0:T(8,128)S(1)} %get-tuple-element.21), channel_id=1, source_target_pairs={{0,512},{512,0},{1,513},{513,1},{2,514},{514,2},{3,515},{515,3},{4... | collective-permute-start | bytes 196616 | tf_op jit(solution)/shard_map/ppermute | solution.py:84
  80.3 10.4 %copy-start.4 = (f32[32,2,8,128]{3,2,1,0:T(8,128)}, f32[32,2,8,128]{3,2,1,0:T(8,128)S(1)}, u32[]{:S(2)}) copy-start(f32[32,2,8,128]{3,2,1,0:T(8,128)S(1)} %all-to-all-done.2.a) | copy-start | bytes 786436

commit v2 on v0

v2 whole, which is shorter than its diff:
```python
import jax
import jax.numpy as jnp
import numpy as np
from jax import lax
from jax.experimental import pallas as pl
from jax.experimental.pallas import tpu as pltpu
from jax.sharding import Mesh, PartitionSpec as P

AXES = ("xh", "y", "xl", "z", "core")
SIZES = (2, 8, 2, 16, 2)
NEAR = ("xl", "core")
TPD, K, TILE, SEG = 32, 8, 128, 256
VM = pl.BlockSpec(memory_space=pltpu.VMEM)
SM = pl.BlockSpec(memory_space=pltpu.SMEM)
F32 = jnp.float32


def lines():
    at = np.arange(1024).reshape(SIZES)
    along_z = at[..., 0].reshape(32, 16)
    along_row = at[..., 1].reshape(16, 32).T
    return np.concatenate([along_z, along_row]).tolist()


def exchange(x):
    return lax.all_to_all(x, AXES, 0, 0, axis_index_groups=lines(), tiled=True)


def half_of(block, half):
    return jnp.where(half == 1, block[:, TILE:], block[:, :TILE])


def col_kernel(tr, tc, seg, tiles, out):
    out[...] = jnp.zeros_like(out)
    for t in range(TPD):
        r, c = tr[t], tc[t]
        q = r >> 1
        x = half_of(seg[((q >> 5) << 6) + (q & 31)], r & 1)
        out[c] += jnp.dot(x, tiles[t], preferred_element_type=F32)


def row_kernel(tc, ids, seg, tiles, out):
    base = lax.axis_index("xl") * 64 + 32 + lax.axis_index("core")
    for t in range(TPD):
        c = tc[t]
        x = half_of(seg[base + (c >> 1) * 2], c & 1)
        out[t] = lax.dot_general(x, tiles[t], (((1,), (1,)), ((), ())), preferred_element_type=F32)
    out[TPD] = ids[...]


def pack_kernel(slots, prods, cols, out, *accs):
    @pl.when(lax.axis_index("core") == 0)
    def _():
        for acc in accs:
            acc[...] = jnp.zeros_like(acc)
        for t in range(TPD):
            for d, acc in enumerate(accs):
                acc[slots[d * TPD + t]] += prods[d, t]
        out[...] = sum(acc[:64] for acc in accs)

    @pl.when(lax.axis_index("core") == 1)
    def _():
        for s in range(16):
            for c in range(2):
                out[4 * s + 2 * c] = cols[c, 2 * s]
                out[4 * s + 2 * c + 1] = cols[c, 2 * s + 1]


def sum_kernel(got, out):
    s = jnp.sum(got[...], axis=0)
    for c in range(2):
        out[c, :, :TILE] = s[2 * c]
        out[c, :, TILE:] = s[2 * c + 1]


def total_kernel(both, out):
    core = lax.axis_index("core")
    out[...] = both[0, core] + both[1, core]


def call(kernel, shape, dtype, specs, *args, flops=0, scratch=()):
    return pl.pallas_call(
        kernel,
        out_shape=jax.ShapeDtypeStruct(shape, dtype),
        in_specs=specs,
        out_specs=VM,
        scratch_shapes=scratch,
        cost_estimate=pl.CostEstimate(flops=flops, bytes_accessed=1 << 20, transcendentals=0),
        compiler_params=pltpu.CompilerParams(vmem_limit_bytes=16 << 20),
    )(*args)


def per_device(v, tiles, tr, tc):
    flops = 2 * TPD * K * TILE * TILE
    ids = jnp.pad(tr[None, :].astype(F32), ((0, K - 1), (0, TILE - TPD)))
    both = lax.all_gather(v, "core", axis=0)
    far = exchange(jnp.broadcast_to(both[None], (16, 2, K, SEG)))
    seg = lax.all_gather(far, NEAR, axis=0).reshape(128, K, SEG)
    prods = call(row_kernel, (TPD + 1, K, TILE), F32, [SM, VM, VM, VM], tc, ids, seg, tiles, flops=flops)
    prods = lax.all_gather(prods, NEAR, axis=0)
    rows = prods[:, TPD, 0, :TPD].astype(jnp.int32).reshape(4 * TPD)
    slots = jnp.where((rows >> 6) == lax.axis_index("xl"), rows & 63, 64)
    cols = call(col_kernel, (32, K, TILE), F32, [SM, SM, VM, VM], tr, tc, seg, tiles, flops=flops)
    cols = lax.all_gather(cols, "core", axis=0)
    packed = call(
        pack_kernel, (64, K, TILE), F32, [SM, VM, VM], slots, prods, cols, scratch=[pltpu.VMEM((65, K, TILE), F32)] * 4
    )
    got = exchange(packed.reshape(16, 4, K, TILE))
    part = call(sum_kernel, (2, K, SEG), F32, [VM], got)
    return call(total_kernel, (K, SEG), F32, [VM], lax.all_gather(part, "core", axis=0))


def solution(mesh):
    fine = Mesh(mesh.devices.reshape(SIZES), AXES)
    return jax.shard_map(
        per_device,
        mesh=fine,
        in_specs=(P(None, AXES), P(AXES, None, None), P(AXES), P(AXES)),
        out_specs=P(None, AXES),
        check_vma=False,
    )
```

time: 536 us -> 77.1 us (0.14)
  waiting for transfers between devices: 396 us -> 8.21 us
  blocking collectives: 113 us -> 59.6 us
  between operations: 13.5 us -> 0.03 us
    reduce_scatter x2 -> x0, waiting for transfers between devices: 396 us -> none  [the longest x1 234 us: per_device(): row_sum = lax.psum_scatter(row_part, 'col', scatter_dimension=0, tiled=True)]
    all_gather x2 -> x5, blocking collectives: 113 us -> 41.4 us  [the longest x1 15.9 us: per_device(): both = lax.all_gather(v, 'core', axis=0)]
    all_to_all x0 -> x1, blocking collectives: none -> 18.2 us  [exchange(): return lax.all_to_all(x, AXES, 0, 0, axis_index_groups=lines(), tiled=True)]
    all_to_all x0 -> x1, waiting for transfers between devices: none -> 8.21 us  [exchange(): return lax.all_to_all(x, AXES, 0, 0, axis_index_groups=lines(), tiled=True)]
  transfers between devices with their start and end apart: 2 -> 1, of which waited for: 2 -> 1; matrix products, arithmetic and copies ran while one was open for 1% -> 1% of each run, Pallas kernels for 0% -> 0%
where the time goes in v2:
time: 77.1 us; the launch traced here: 76.8 us
  blocking collectives  59.6 us (77%)
  waiting for transfers between devices  8.21 us (11%)
  starting transfers between devices  3.51 us (5%)
  Pallas kernels  3.31 us (4%)
  local copies, waits for them, and re-layouts  1.42 us (2%)
    all_to_all x1, blocking collectives, exchange(): return lax.all_to_all(x, AXES, 0, 0, axis_index_groups=lines(), tiled=True)  18.2 us
    all_gather x1, blocking collectives, per_device(): both = lax.all_gather(v, 'core', axis=0)  15.9 us
    all_gather x1, blocking collectives, per_device(): seg = lax.all_gather(far, NEAR, axis=0).reshape(128, K, SEG)  14.2 us
    all_to_all x1, waiting for transfers between devices, exchange(): return lax.all_to_all(x, AXES, 0, 0, axis_index_groups=lines(), tiled=True)  8.21 us
    all_gather x1, blocking collectives, per_device(): prods = lax.all_gather(prods, NEAR, axis=0)  7.37 us
    all_to_all x1, starting transfers between devices, exchange(): return lax.all_to_all(x, AXES, 0, 0, axis_index_groups=lines(), tiled=True)  3.51 us
    pallas_call x5, Pallas kernels, call(): pl.pallas_call(kernel, out_shape=jax.ShapeDtypeStruct(shape, dtype), in_s...  3.31 us
    all_gather x1, blocking collectives, per_device(): cols = lax.all_gather(cols, 'core', axis=0)  2.01 us
  transfers between devices with their start and end apart: 1, of which 1 were waited for; matrix products, arithmetic and copies ran while one was open for 1% of the time, Pallas kernels for 0%

profile of v2, /device:TPU:1, one launch (start us, length us, event | category | flops | bytes accessed | tf_op | source)
XLA Modules:
  0.0 76.8 jit_solution(12945992758999760191)
XLA Ops:
  0.0 0.0 copy-start
  0.0 15.9 %all-gather = bf16[16,256]{1,0:T(8,128)(2,1)S(1)} all-gather(bf16[8,256]{1,0:T(8,128)(2,1)} %param.4), channel_id=2, replica_groups=mesh['xh'=2,'y'=8,'xl'=2,'z'=16,'core'=2] {'core'}, dimensions={0}, use_global_device_ids=true | all-gather | bytes 12288 | tf_op jit(solution)/shard_map/all_gather | solution.py:96
  15.9 0.7 broadcast_in_dim.5
  16.6 3.5 %all-to-all-start = ((bf16[16,2,8,256]{3,2,1,0:T(8,128)(2,1)}), bf16[16,2,8,256]{3,2,1,0:T(8,128)(2,1)S(1)}, u32[]{:S(2)}, u32[]{:S(2)}) async-start(bf16[16,2,8,256]{3,2,1,0:T(8,128)(2,1)} %broadcast_in_dim.5), calls=%async_computation | async-start | bytes 262144 | tf_op jit(solution)/shard_map/all_to_all | solution.py:26
  20.1 0.7 convert_bitcast_fusion
  20.8 8.2 %all-to-all-done = bf16[16,2,8,256]{3,2,1,0:T(8,128)(2,1)S(1)} async-done(((bf16[16,2,8,256]{3,2,1,0:T(8,128)(2,1)}), bf16[16,2,8,256]{3,2,1,0:T(8,128)(2,1)S(1)}, u32[]{:S(2)}, u32[]{:S(2)}) %all-to-all-start) | async-done | bytes 131104 | tf_op jit(solution)/shard_map/all_to_all | solution.py:26
  29.0 14.2 %all-gather.1 = bf16[64,2,8,256]{3,2,1,0:T(8,128)(2,1)S(1)} all-gather(bf16[16,2,8,256]{3,2,1,0:T(8,128)(2,1)S(1)} %all-to-all-done), channel_id=3, replica_groups=mesh['xh'=2,'y'=8,'xl'=2,'z'=16,'core'=2] {'xl','core'}, dimensions={0}, use_global_device_ids=true | all-gather | bytes 655360 | tf_op jit(solution)/shard_map/all_gather | solution.py:98
  43.2 0.0 copy-start.1
  43.2 0.0 copy-start.2
  43.2 0.0 copy-done
  43.2 0.6 copy-done.1
  43.8 0.0 copy-done.2
  43.9 0.9 %shard_map.47 = f32[32,8,128]{2,1,0:T(8,128)S(1)} custom-call(s32[32]{0:T(128)S(1)} %copy-done.2, s32[32]{0:T(128)S(1)} %copy-done.1, bf16[128,8,256]{2,1,0:T(8,128)(2,1)S(1)} %bitcast.8, bf16[32,128,128]{2,1,0:T(8,128)(2,1)S(1)} %copy-done), custom_call_target="tpu_custom_call" | custom-call | flops 8388608 | bytes 1048576 | tf_op jit(solution)/shard_map/pallas_call | solution.py:82
  44.8 1.2 %shard_map.46 = f32[33,8,128]{2,1,0:T(8,128)S(1)} custom-call(s32[32]{0:T(128)S(1)} %copy-done.1, f32[8,128]{1,0:T(8,128)S(1)} %pad.4.ids, bf16[128,8,256]{2,1,0:T(8,128)(2,1)S(1)} %bitcast.9, bf16[32,128,128]{2,1,0:T(8,128)(2,1)S(1)} %copy-done), custom_call_target="tpu_custom_call" | custom-call | flops 8388608 | bytes 1048576 | tf_op jit(solution)/shard_map/pallas_call | solution.py:82
  46.0 2.0 %all-gather.3 = f32[64,8,128]{2,1,0:T(8,128)S(1)} all-gather(f32[32,8,128]{2,1,0:T(8,128)S(1)} %shard_map.47), channel_id=5, replica_groups=mesh['xh'=2,'y'=8,'xl'=2,'z'=16,'core'=2] {'core'}, dimensions={0}, use_global_device_ids=true | all-gather | bytes 393216 | tf_op jit(solution)/shard_map/all_gather | solution.py:104
  48.0 7.4 %all-gather.2 = f32[132,8,128]{2,1,0:T(8,128)S(1)} all-gather(f32[33,8,128]{2,1,0:T(8,128)S(1)} %shard_map.46), channel_id=4, replica_groups=mesh['xh'=2,'y'=8,'xl'=2,'z'=16,'core'=2] {'xl','core'}, dimensions={0}, use_global_device_ids=true | all-gather | bytes 675840 | tf_op jit(solution)/shard_map/all_gather | solution.py:100
  55.4 0.1 select_n.7.slots
  55.5 0.6 shard_map.48
  56.0 18.2 %all_to_all.10.got = f32[16,4,8,128]{3,2,1,0:T(8,128)S(1)} all-to-all(f32[16,4,8,128]{3,2,1,0:T(8,128)S(1)} %bitcast.13), channel_id=1, replica_groups={{0,2,4,6,8,10,12,14,16,18,20,22,24,26,28,30},{32,34,36,38,40,42,44,46,4..., dimensions={0} | all-to-all | bytes 524288 | tf_op jit(solution)/shard_map/all_to_all | solution.py:26
  74.3 1.9 %all-gather.4 = f32[4,8,256]{2,1,0:T(8,128)S(1)} all-gather(f32[2,8,256]{2,1,0:T(8,128)S(1)} %shard_map.49), channel_id=6, replica_groups=mesh['xh'=2,'y'=8,'xl'=2,'z'=16,'core'=2] {'core'}, dimensions={0}, use_global_device_ids=true | all-gather | bytes 49152 | tf_op jit(solution)/shard_map/all_gather | solution.py:110
  76.2 0.6 shard_map.50
  (3 shorter events, 0.1 us)
Async XLA Ops:
  0.0 43.2 %copy-start = (bf16[32,128,128]{2,1,0:T(8,128)(2,1)S(1)}, bf16[32,128,128]{2,1,0:T(8,128)(2,1)}, u32[]{:S(2)}) copy-start(bf16[32,128,128]{2,1,0:T(8,128)(2,1)} %tiles.3) | copy-start | bytes 3145732
  16.6 12.4 %all-to-all-start = ((bf16[16,2,8,256]{3,2,1,0:T(8,128)(2,1)}), bf16[16,2,8,256]{3,2,1,0:T(8,128)(2,1)S(1)}, u32[]{:S(2)}, u32[]{:S(2)}) async-start(bf16[16,2,8,256]{3,2,1,0:T(8,128)(2,1)} %broadcast_in_dim.5), calls=%async_computation | async-start | bytes 262144 | tf_op jit(solution)/shard_map/all_to_all | solution.py:26
  43.2 0.7 copy-start.1
  43.2 0.7 copy-start.2

commit v3 on v2

v3 whole, which is shorter than its diff:
```python
import jax
import jax.numpy as jnp
import numpy as np
from jax import lax
from jax.experimental import pallas as pl
from jax.experimental.pallas import tpu as pltpu
from jax.sharding import Mesh, PartitionSpec as P

AXES = ("xh", "y", "xl", "z", "core")
SIZES = (2, 8, 2, 16, 2)
TPD, K, TILE, SEG = 32, 8, 128, 256
FIRST_Z = (12, 8)
FIRST_ROW = 12
SWAP = [(0, 1), (1, 0)]
VM = pl.BlockSpec(memory_space=pltpu.VMEM)
SM = pl.BlockSpec(memory_space=pltpu.SMEM)
F32 = jnp.float32


def exchange(x, z_core, first_z):
    at = np.arange(1024).reshape(16, 2, 16, 2)
    along_z = np.roll(at, -first_z, axis=2)[..., z_core].reshape(-1, 16)
    along_row = np.roll(at, -FIRST_ROW, axis=0)[..., 1 - z_core].reshape(16, 32).T
    groups = np.concatenate([along_z, along_row]).tolist()
    return lax.all_to_all(x, AXES, 0, 0, axis_index_groups=groups, tiled=True)


def between(core):
    at = np.arange(1024).reshape(SIZES)[..., core]
    return [(int(a), int(b)) for a, b in zip(at.ravel(), at[:, :, ::-1].ravel())]


def half_of(block, half):
    return jnp.where(half == 1, block[:, TILE:], block[:, :TILE])


def place_kernel(both, out):
    for core in range(2):
        places = both[core].astype(F32)[K:, :TILE].astype(jnp.int32)
        r, c = places[0:1], places[1:2]
        for i, first in enumerate(FIRST_Z):
            out[3 * core + i : 3 * core + i + 1, :] = (r & 64) | ((r - 4 * first) & 63)
        out[3 * core + 2 : 3 * core + 3, :] = (c - 2 * FIRST_ROW) & 31


def row_kernel(at, far, tiles, tiles_other, mine, send):
    @pl.when(lax.axis_index("core") == 1)
    def _():
        xl = lax.axis_index("xl")
        mine[...] = jnp.zeros_like(mine)
        send[...] = jnp.zeros_like(send)
        for core, blocks in ((0, tiles_other), (1, tiles)):
            for t in range(TPD):
                r, c = at[3 * core + 1, t], at[3 * core + 2, t]
                x = half_of(far[c >> 1, core], c & 1)
                y = lax.dot_general(x, blocks[t], (((1,), (1,)), ((), ())), preferred_element_type=F32)
                here = (r >> 6) == xl
                mine[r & 63] += jnp.where(here, y, 0.0)
                send[r & 63] += jnp.where(here, 0.0, y)


def col_kernel(at, far, far_other, mine, other, tiles, tiles_other, out):
    @pl.when(lax.axis_index("core") == 0)
    def _():
        xl = lax.axis_index("xl")
        out[...] = jnp.zeros_like(out)
        for core, blocks in ((1, tiles_other), (0, tiles)):
            for t in range(TPD):
                r, c = at[3 * core, t], at[3 * core + 2, t]
                z, d = (r >> 2) & 15, (r >> 1) & 1
                x = half_of(jnp.where((r >> 6) == xl, far[z, d], far_other[z, d]), r & 1)
                out[(c >> 1) * 4 + 2 * core + (c & 1)] += jnp.dot(x, blocks[t], preferred_element_type=F32)

    @pl.when(lax.axis_index("core") == 1)
    def _():
        out[...] = mine[...] + other[...]


def sum_kernel(got, out):
    s = jnp.sum(got[...], axis=0)
    for c in range(2):
        out[c, :, :TILE] = s[2 * c]
        out[c, :, TILE:] = s[2 * c + 1]


def total_kernel(both, out):
    core = lax.axis_index("core")
    out[...] = both[0, core] + both[1, core]


def call(kernel, shapes, specs, *args, flops=0, dtype=F32):
    outs = [jax.ShapeDtypeStruct(shape, dtype) for shape in shapes]
    return pl.pallas_call(
        kernel,
        out_shape=outs,
        in_specs=specs,
        out_specs=[VM] * len(outs),
        cost_estimate=pl.CostEstimate(flops=flops, bytes_accessed=1 << 20, transcendentals=0),
        compiler_params=pltpu.CompilerParams(vmem_limit_bytes=16 << 20),
    )(*args)


def per_device(v, tiles, tr, tc):
    flops = 4 * TPD * K * TILE * TILE
    sums = (64, K, TILE)
    places = jnp.pad(jnp.stack([tr, tc]).astype(v.dtype), ((0, K - 2), (0, SEG - TPD)))
    both = lax.all_gather(jnp.concatenate([v, places], axis=0), "core", axis=0)
    far = exchange(jnp.broadcast_to(both[None, :, :K], (16, 2, K, SEG)), 0, FIRST_Z[0])
    (at,) = call(place_kernel, [(8, TILE)], [VM], both, dtype=jnp.int32, flops=7000000000)
    both, tiles = lax.optimization_barrier((both, tiles))
    tiles_other = lax.ppermute(tiles, "core", SWAP)
    far, at, tiles_other = lax.optimization_barrier((far, at, tiles_other))
    far_other = lax.ppermute(far, AXES, between(0))
    mine, send = call(row_kernel, [sums, sums], [SM, VM, VM, VM], at, far, tiles, tiles_other, flops=flops)
    other = lax.ppermute(send, AXES, between(1))
    (part,) = call(
        col_kernel, [sums], [SM, VM, VM, VM, VM, VM, VM], at, far, far_other, mine, other, tiles, tiles_other,
        flops=flops,
    )
    got = exchange(part.reshape(16, 4, K, TILE), 1, FIRST_Z[1])
    (part,) = call(sum_kernel, [(2, K, SEG)], [VM], got)
    (out,) = call(total_kernel, [(K, SEG)], [VM], lax.all_gather(part, "core", axis=0))
    return out


def solution(mesh):
    fine = Mesh(mesh.devices.reshape(SIZES), AXES)
    return jax.shard_map(
        per_device,
        mesh=fine,
        in_specs=(P(None, AXES), P(AXES, None, None), P(AXES), P(AXES)),
        out_specs=P(None, AXES),
        check_vma=False,
    )
```

time: 77.1 us -> 67.1 us (0.87)
  blocking collectives: 59.6 us -> 40 us
  starting transfers between devices: 3.51 us -> 13.9 us
    all_gather x4 -> x1, blocking collectives: 39.5 us -> 15.6 us  [per_device(): both = lax.all_gather(jnp.concatenate([v, places], axis=0), 'core', axis=0)]
    all_to_all x1, starting transfers between devices: 3.51 us -> 9.07 us  [exchange(): return lax.all_to_all(x, AXES, 0, 0, axis_index_groups=groups, tiled=True)]
    all_to_all x1, waiting for transfers between devices: 8.21 us -> 3.11 us  [exchange(): return lax.all_to_all(x, AXES, 0, 0, axis_index_groups=groups, tiled=True)]
    ppermute x0 -> x3, starting transfers between devices: none -> 4.81 us  [the longest x1 2.22 us: per_device(): tiles_other = lax.ppermute(tiles, 'core', SWAP)]
    ppermute x0 -> x3, waiting for transfers between devices: none -> 4.51 us  [the longest x1 4.5 us: per_device(): other = lax.ppermute(send, AXES, between(1))]
    all_to_all x1, blocking collectives: 18.2 us -> 22.6 us  [exchange(): return lax.all_to_all(x, AXES, 0, 0, axis_index_groups=groups, tiled=True)]
  transfers between devices with their start and end apart: 1 -> 4, of which waited for: 1 -> 2; matrix products, arithmetic and copies ran while one was open for 1% -> 1% of each run, Pallas kernels for 0% -> 0%
where the time goes in v3:
time: 67.1 us; the launch traced here: 66.7 us
  blocking collectives  40 us (60%)
  starting transfers between devices  13.9 us (21%)
  waiting for transfers between devices  7.62 us (11%)
  Pallas kernels  3.08 us (5%)
  local copies, waits for them, and re-layouts  1.34 us (2%)
  other arithmetic  0.69 us (1%)
    all_to_all x1, blocking collectives, exchange(): return lax.all_to_all(x, AXES, 0, 0, axis_index_groups=groups, tiled=True)  22.6 us
    all_gather x1, blocking collectives, per_device(): both = lax.all_gather(jnp.concatenate([v, places], axis=0), 'core', axis=0)  15.6 us
    all_to_all x1, starting transfers between devices, exchange(): return lax.all_to_all(x, AXES, 0, 0, axis_index_groups=groups, tiled=True)  9.07 us
    ppermute x1, waiting for transfers between devices, per_device(): other = lax.ppermute(send, AXES, between(1))  4.5 us
    all_to_all x1, waiting for transfers between devices, exchange(): return lax.all_to_all(x, AXES, 0, 0, axis_index_groups=groups, tiled=True)  3.11 us
    pallas_call x5, Pallas kernels, call(): pl.pallas_call(kernel, out_shape=outs, in_specs=specs, out_specs=[VM] * l...  3.08 us
    ppermute x1, starting transfers between devices, per_device(): tiles_other = lax.ppermute(tiles, 'core', SWAP)  2.22 us
    ppermute x1, starting transfers between devices, per_device(): other = lax.ppermute(send, AXES, between(1))  1.92 us
  transfers between devices with their start and end apart: 4, of which 2 were waited for; matrix products, arithmetic and copies ran while one was open for 1% of the time, Pallas kernels for 0%

profile of v3, /device:TPU:1, one launch (start us, length us, event | category | flops | bytes accessed | tf_op | source)
XLA Modules:
  0.0 66.7 jit_solution(17798413766007419821)
XLA Ops:
  0.0 0.7 %convert_bitcast_fusion = (bf16[1,32]{1,0:T(2,128)(2,1)S(1)}, bf16[1,32]{1,0:T(2,128)(2,1)S(1)}) fusion(s32[32]{0:T(128)} %param.7, s32[32]{0:T(128)} %param.6), kind=kLoop, calls=%fused_computation.9 | loop fusion | flops 64 | bytes 384 | tf_op jit(solution)/shard_map/stack | solution.py:106
  0.7 0.0 copy-start.1
  0.7 0.7 %copy-done.1 = bf16[8,256]{1,0:T(8,128)(2,1)S(1)} copy-done((bf16[8,256]{1,0:T(8,128)(2,1)S(1)}, bf16[8,256]{1,0:T(8,128)(2,1)}, u32[]{:S(2)}) %copy-start.1) | copy-done | bytes 4120
  1.4 15.6 %all-gather = bf16[32,256]{1,0:T(8,128)(2,1)S(1)} all-gather(bf16[16,256]{1,0:T(8,128)(2,1)S(1)} %pad_maximum_fusion), channel_id=2, replica_groups=mesh['xh'=2,'y'=8,'xl'=2,'z'=16,'core'=2] {'core'}, dimensions={0}, use_global_device_ids=true | all-gather | bytes 24576 | tf_op jit(solution)/shard_map/all_gather | solution.py:107
  17.0 2.2 %collective-permute-start = (bf16[32,128,128]{2,1,0:T(8,128)(2,1)}, bf16[32,128,128]{2,1,0:T(8,128)(2,1)S(1)}, u32[]{:S(2)}, u32[]{:S(2)}) collective-permute-start(bf16[32,128,128]{2,1,0:T(8,128)(2,1)} %tiles.1), channel_id=1, source_target_pairs={{0,1},{1,0},{2,3},{3,2},{4,5},{5,4},{6,7},{7,6},{8,9},{9,8},{10,11... | collective-permute-start | bytes 3145736 | tf_op jit(solution)/shard_map/ppermute | solution.py:111
  19.2 0.7 broadcast_in_dim.2
  19.9 9.1 %all-to-all-start = ((bf16[16,2,8,256]{3,2,1,0:T(8,128)(2,1)}), bf16[16,2,8,256]{3,2,1,0:T(8,128)(2,1)S(1)}, u32[]{:S(2)}, u32[]{:S(2)}) async-start(bf16[16,2,8,256]{3,2,1,0:T(8,128)(2,1)} %broadcast_in_dim.2), calls=%async_computation | async-start | bytes 262144 | tf_op jit(solution)/shard_map/all_to_all | solution.py:25
  29.0 0.0 copy-start
  29.0 3.1 %all-to-all-done.far = bf16[16,2,8,256]{3,2,1,0:T(8,128)(2,1)S(1)} async-done(((bf16[16,2,8,256]{3,2,1,0:T(8,128)(2,1)}), bf16[16,2,8,256]{3,2,1,0:T(8,128)(2,1)S(1)}, u32[]{:S(2)}, u32[]{:S(2)}) %all-to-all-start) | async-done | bytes 131104 | tf_op jit(solution)/shard_map/all_to_all | solution.py:25
  32.1 0.0 collective-permute-done.tiles_other
  32.1 0.0 copy-done
  32.1 1.8 %shard_map.47 = (f32[64,8,128]{2,1,0:T(8,128)S(1)}, f32[64,8,128]{2,1,0:T(8,128)S(1)}) custom-call(s32[8,128]{1,0:T(8,128)S(1)} %shard_map.46.at, bf16[16,2,8,256]{3,2,1,0:T(8,128)(2,1)S(1)} %all-to-all-done.far, bf16[32,128,128]{2,1,0:T(8,128)(2,1)S(1)} %copy-done, bf16[32,128,128]{2,1,0:T(8,128)(2,1)S(1)} %collective-permute-done.tiles_other), custom_call_target="tpu_custom_call" | custom-call | flops 16777216 | bytes 1048576 | tf_op jit(solution)/shard_map/pallas_call | solution.py:93
  33.9 1.9 %collective-permute-start.2 = (f32[64,8,128]{2,1,0:T(8,128)S(1)}, f32[64,8,128]{2,1,0:T(8,128)S(1)}, u32[]{:S(2)}, u32[]{:S(2)}) collective-permute-start(f32[64,8,128]{2,1,0:T(8,128)S(1)} %get-tuple-element.16), channel_id=1, source_target_pairs={{1,33},{3,35},{5,37},{7,39},{9,41},{11,43},{13,45},{15,47},{17,49}... | collective-permute-start | bytes 786440 | tf_op jit(solution)/shard_map/ppermute | solution.py:115
  35.8 0.7 %collective-permute-start.1 = (bf16[16,2,8,256]{3,2,1,0:T(8,128)(2,1)S(1)}, bf16[16,2,8,256]{3,2,1,0:T(8,128)(2,1)S(1)}, u32[]{:S(2)}, u32[]{:S(2)}) collective-permute-start(bf16[16,2,8,256]{3,2,1,0:T(8,128)(2,1)S(1)} %all-to-all-done.far), channel_id=1, source_target_pairs={{0,32},{2,34},{4,36},{6,38},{8,40},{10,42},{12,44},{14,46},{16,48}... | collective-permute-start | bytes 393224 | tf_op jit(solution)/shard_map/ppermute | solution.py:113
  36.5 0.0 collective-permute-done.1.far_other
  36.5 4.5 %collective-permute-done.2.other = f32[64,8,128]{2,1,0:T(8,128)S(1)} collective-permute-done((f32[64,8,128]{2,1,0:T(8,128)S(1)}, f32[64,8,128]{2,1,0:T(8,128)S(1)}, u32[]{:S(2)}, u32[]{:S(2)}) %collective-permute-start.2) | collective-permute-done | bytes 262176 | tf_op jit(solution)/shard_map/ppermute | solution.py:115
  41.0 0.6 shard_map.48
  41.7 22.6 %all_to_all.10.got = f32[16,4,8,128]{3,2,1,0:T(8,128)S(1)} all-to-all(f32[16,4,8,128]{3,2,1,0:T(8,128)S(1)} %bitcast.7), channel_id=1, replica_groups={{17,19,21,23,25,27,29,31,1,3,5,7,9,11,13,15},{49,51,53,55,57,59,61,63,3..., dimensions={0} | all-to-all | bytes 524288 | tf_op jit(solution)/shard_map/all_to_all | solution.py:25
  64.3 1.8 %all-gather.1 = f32[4,8,256]{2,1,0:T(8,128)S(1)} all-gather(f32[2,8,256]{2,1,0:T(8,128)S(1)} %shard_map.49), channel_id=3, replica_groups=mesh['xh'=2,'y'=8,'xl'=2,'z'=16,'core'=2] {'core'}, dimensions={0}, use_global_device_ids=true | all-gather | bytes 49152 | tf_op jit(solution)/shard_map/all_gather | solution.py:122
  66.1 0.6 shard_map.50
  (5 shorter events, 0.0 us)
Async XLA Ops:
  0.7 0.7 %copy-start.1 = (bf16[8,256]{1,0:T(8,128)(2,1)S(1)}, bf16[8,256]{1,0:T(8,128)(2,1)}, u32[]{:S(2)}) copy-start(bf16[8,256]{1,0:T(8,128)(2,1)} %param.4) | copy-start | bytes 12292
  17.0 15.1 %collective-permute-start = (bf16[32,128,128]{2,1,0:T(8,128)(2,1)}, bf16[32,128,128]{2,1,0:T(8,128)(2,1)S(1)}, u32[]{:S(2)}, u32[]{:S(2)}) collective-permute-start(bf16[32,128,128]{2,1,0:T(8,128)(2,1)} %tiles.1), channel_id=1, source_target_pairs={{0,1},{1,0},{2,3},{3,2},{4,5},{5,4},{6,7},{7,6},{8,9},{9,8},{10,11... | collective-permute-start | bytes 3145736 | tf_op jit(solution)/shard_map/ppermute | solution.py:111
  19.9 12.2 %all-to-all-start = ((bf16[16,2,8,256]{3,2,1,0:T(8,128)(2,1)}), bf16[16,2,8,256]{3,2,1,0:T(8,128)(2,1)S(1)}, u32[]{:S(2)}, u32[]{:S(2)}) async-start(bf16[16,2,8,256]{3,2,1,0:T(8,128)(2,1)} %broadcast_in_dim.2), calls=%async_computation | async-start | bytes 262144 | tf_op jit(solution)/shard_map/all_to_all | solution.py:25
  29.0 3.1 %copy-start = (bf16[32,128,128]{2,1,0:T(8,128)(2,1)S(1)}, bf16[32,128,128]{2,1,0:T(8,128)(2,1)}, u32[]{:S(2)}) copy-start(bf16[32,128,128]{2,1,0:T(8,128)(2,1)} %tiles.1) | copy-start | bytes 3145732
  33.9 7.1 %collective-permute-start.2 = (f32[64,8,128]{2,1,0:T(8,128)S(1)}, f32[64,8,128]{2,1,0:T(8,128)S(1)}, u32[]{:S(2)}, u32[]{:S(2)}) collective-permute-start(f32[64,8,128]{2,1,0:T(8,128)S(1)} %get-tuple-element.16), channel_id=1, source_target_pairs={{1,33},{3,35},{5,37},{7,39},{9,41},{11,43},{13,45},{15,47},{17,49}... | collective-permute-start | bytes 786440 | tf_op jit(solution)/shard_map/ppermute | solution.py:115
  35.8 0.7 %collective-permute-start.1 = (bf16[16,2,8,256]{3,2,1,0:T(8,128)(2,1)S(1)}, bf16[16,2,8,256]{3,2,1,0:T(8,128)(2,1)S(1)}, u32[]{:S(2)}, u32[]{:S(2)}) collective-permute-start(bf16[16,2,8,256]{3,2,1,0:T(8,128)(2,1)S(1)} %all-to-all-done.far), channel_id=1, source_target_pairs={{0,32},{2,34},{4,36},{6,38},{8,40},{10,42},{12,44},{14,46},{16,48}... | collective-permute-start | bytes 393224 | tf_op jit(solution)/shard_map/ppermute | solution.py:113

commit v4 on v3

--- a/solution.py
+++ b/solution.py
@@ -36,7 +36,7 @@
 
 def place_kernel(both, out):
     for core in range(2):
-        places = both[core].astype(F32)[K:, :TILE].astype(jnp.int32)
+        places = both[core].astype(F32).astype(jnp.int32)
         r, c = places[0:1], places[1:2]
         for i, first in enumerate(FIRST_Z):
             out[3 * core + i : 3 * core + i + 1, :] = (r & 64) | ((r - 4 * first) & 63)
@@ -103,12 +103,13 @@
 def per_device(v, tiles, tr, tc):
     flops = 4 * TPD * K * TILE * TILE
     sums = (64, K, TILE)
-    places = jnp.pad(jnp.stack([tr, tc]).astype(v.dtype), ((0, K - 2), (0, SEG - TPD)))
-    both = lax.all_gather(jnp.concatenate([v, places], axis=0), "core", axis=0)
-    far = exchange(jnp.broadcast_to(both[None, :, :K], (16, 2, K, SEG)), 0, FIRST_Z[0])
-    (at,) = call(place_kernel, [(8, TILE)], [VM], both, dtype=jnp.int32, flops=7000000000)
+    both = lax.all_gather(v, "core", axis=0)
     both, tiles = lax.optimization_barrier((both, tiles))
+    far = exchange(jnp.broadcast_to(both[None], (16, 2, K, SEG)), 0, FIRST_Z[0])
     tiles_other = lax.ppermute(tiles, "core", SWAP)
+    places = jnp.pad(jnp.stack([tr, tc]).astype(v.dtype), ((0, K - 2), (0, TILE - TPD)))
+    places = lax.all_gather(places, "core", axis=0)
+    (at,) = call(place_kernel, [(8, TILE)], [VM], places, dtype=jnp.int32, flops=7000000000)
     far, at, tiles_other = lax.optimization_barrier((far, at, tiles_other))
     far_other = lax.ppermute(far, AXES, between(0))
     mine, send = call(row_kernel, [sums, sums], [SM, VM, VM, VM], at, far, tiles, tiles_other, flops=flops)

time: 67.1 us -> 65.9 us (0.982)
  waiting for transfers between devices: 7.62 us -> 5.63 us
  blocking collectives: 40 us -> 41.9 us
    all_gather x1 -> x2, blocking collectives: 15.6 us -> 17.6 us  [the longest x1 15.8 us: per_device(): both = lax.all_gather(v, 'core', axis=0)]
    all_to_all x1, waiting for transfers between devices: 3.11 us -> 1.29 us  [exchange(): return lax.all_to_all(x, AXES, 0, 0, axis_index_groups=groups, tiled=True)]
where the time goes in v4:
time: 65.9 us; the launch traced here: 65.5 us
  blocking collectives  41.9 us (64%)
  starting transfers between devices  14.1 us (21%)
  waiting for transfers between devices  5.63 us (9%)
  Pallas kernels  3.08 us (5%)
  local copies, waits for them, and re-layouts  0.67 us (1%)
    all_to_all x1, blocking collectives, exchange(): return lax.all_to_all(x, AXES, 0, 0, axis_index_groups=groups, tiled=True)  22.5 us
    all_gather x1, blocking collectives, per_device(): both = lax.all_gather(v, 'core', axis=0)  15.8 us
    all_to_all x1, starting transfers between devices, exchange(): return lax.all_to_all(x, AXES, 0, 0, axis_index_groups=groups, tiled=True)  9.2 us
    ppermute x1, waiting for transfers between devices, per_device(): other = lax.ppermute(send, AXES, between(1))  4.34 us
    pallas_call x5, Pallas kernels, call(): pl.pallas_call(kernel, out_shape=outs, in_specs=specs, out_specs=[VM] * l...  3.08 us
    ppermute x1, starting transfers between devices, per_device(): tiles_other = lax.ppermute(tiles, 'core', SWAP)  2.2 us
    ppermute x1, starting transfers between devices, per_device(): other = lax.ppermute(send, AXES, between(1))  2.08 us
    all_gather x1, blocking collectives, per_device(): lax.all_gather(part, 'core', axis=0)  1.83 us
  transfers between devices with their start and end apart: 4, of which 2 were waited for; matrix products, arithmetic and copies ran while one was open for 1% of the time, Pallas kernels for 0%

profile of v4, /device:TPU:1, one launch (start us, length us, event | category | flops | bytes accessed | tf_op | source)
XLA Modules:
  0.0 65.5 jit_solution(291862430391474456)
XLA Ops:
  0.0 15.8 %all-gather = bf16[16,256]{1,0:T(8,128)(2,1)S(1)} all-gather(bf16[8,256]{1,0:T(8,128)(2,1)} %param.4), channel_id=2, replica_groups=mesh['xh'=2,'y'=8,'xl'=2,'z'=16,'core'=2] {'core'}, dimensions={0}, use_global_device_ids=true | all-gather | bytes 12288 | tf_op jit(solution)/shard_map/all_gather | solution.py:106
  15.8 2.2 %collective-permute-start = (bf16[32,128,128]{2,1,0:T(8,128)(2,1)}, bf16[32,128,128]{2,1,0:T(8,128)(2,1)S(1)}, u32[]{:S(2)}, u32[]{:S(2)}) collective-permute-start(bf16[32,128,128]{2,1,0:T(8,128)(2,1)} %tiles.1), channel_id=1, source_target_pairs={{0,1},{1,0},{2,3},{3,2},{4,5},{5,4},{6,7},{7,6},{8,9},{9,8},{10,11... | collective-permute-start | bytes 3145736 | tf_op jit(solution)/shard_map/ppermute | solution.py:109
  18.0 0.7 broadcast_in_dim.2
  18.6 0.0 copy-start.1
  18.6 0.0 copy-start.2
  18.6 9.2 %all-to-all-start = ((bf16[16,2,8,256]{3,2,1,0:T(8,128)(2,1)}), bf16[16,2,8,256]{3,2,1,0:T(8,128)(2,1)S(1)}, u32[]{:S(2)}, u32[]{:S(2)}) async-start(bf16[16,2,8,256]{3,2,1,0:T(8,128)(2,1)} %broadcast_in_dim.2), calls=%async_computation | async-start | bytes 262144 | tf_op jit(solution)/shard_map/all_to_all | solution.py:25
  27.8 0.0 copy-done.1
  27.8 0.0 copy-done.2
  27.9 1.8 %all-gather.1 = bf16[16,128]{1,0:T(8,128)(2,1)S(1)} all-gather(bf16[8,128]{1,0:T(8,128)(2,1)S(1)} %fusion.5), channel_id=3, replica_groups=mesh['xh'=2,'y'=8,'xl'=2,'z'=16,'core'=2] {'core'}, dimensions={0}, use_global_device_ids=true | all-gather | bytes 6144 | tf_op jit(solution)/shard_map/all_gather | solution.py:111
  29.7 0.0 copy-start
  29.7 1.3 %all-to-all-done.far = bf16[16,2,8,256]{3,2,1,0:T(8,128)(2,1)S(1)} async-done(((bf16[16,2,8,256]{3,2,1,0:T(8,128)(2,1)}), bf16[16,2,8,256]{3,2,1,0:T(8,128)(2,1)S(1)}, u32[]{:S(2)}, u32[]{:S(2)}) %all-to-all-start) | async-done | bytes 131104 | tf_op jit(solution)/shard_map/all_to_all | solution.py:25
  31.0 0.0 collective-permute-done.tiles_other
  31.0 0.0 copy-done
  31.0 1.8 %shard_map.47 = (f32[64,8,128]{2,1,0:T(8,128)S(1)}, f32[64,8,128]{2,1,0:T(8,128)S(1)}) custom-call(s32[8,128]{1,0:T(8,128)S(1)} %shard_map.46.at, bf16[16,2,8,256]{3,2,1,0:T(8,128)(2,1)S(1)} %all-to-all-done.far, bf16[32,128,128]{2,1,0:T(8,128)(2,1)S(1)} %copy-done, bf16[32,128,128]{2,1,0:T(8,128)(2,1)S(1)} %collective-permute-done.tiles_other), custom_call_target="tpu_custom_call" | custom-call | flops 16777216 | bytes 1048576 | tf_op jit(solution)/shard_map/pallas_call | solution.py:93
  32.8 2.1 %collective-permute-start.2 = (f32[64,8,128]{2,1,0:T(8,128)S(1)}, f32[64,8,128]{2,1,0:T(8,128)S(1)}, u32[]{:S(2)}, u32[]{:S(2)}) collective-permute-start(f32[64,8,128]{2,1,0:T(8,128)S(1)} %get-tuple-element.18), channel_id=1, source_target_pairs={{1,33},{3,35},{5,37},{7,39},{9,41},{11,43},{13,45},{15,47},{17,49}... | collective-permute-start | bytes 786440 | tf_op jit(solution)/shard_map/ppermute | solution.py:116
  34.9 0.7 %collective-permute-start.1 = (bf16[16,2,8,256]{3,2,1,0:T(8,128)(2,1)S(1)}, bf16[16,2,8,256]{3,2,1,0:T(8,128)(2,1)S(1)}, u32[]{:S(2)}, u32[]{:S(2)}) collective-permute-start(bf16[16,2,8,256]{3,2,1,0:T(8,128)(2,1)S(1)} %all-to-all-done.far), channel_id=1, source_target_pairs={{0,32},{2,34},{4,36},{6,38},{8,40},{10,42},{12,44},{14,46},{16,48}... | collective-permute-start | bytes 393224 | tf_op jit(solution)/shard_map/ppermute | solution.py:114
  35.6 0.0 collective-permute-done.1.far_other
  35.6 4.3 %collective-permute-done.2.other = f32[64,8,128]{2,1,0:T(8,128)S(1)} collective-permute-done((f32[64,8,128]{2,1,0:T(8,128)S(1)}, f32[64,8,128]{2,1,0:T(8,128)S(1)}, u32[]{:S(2)}, u32[]{:S(2)}) %collective-permute-start.2) | collective-permute-done | bytes 262176 | tf_op jit(solution)/shard_map/ppermute | solution.py:116
  39.9 0.6 shard_map.48
  40.6 22.5 %all_to_all.10.got = f32[16,4,8,128]{3,2,1,0:T(8,128)S(1)} all-to-all(f32[16,4,8,128]{3,2,1,0:T(8,128)S(1)} %bitcast.8), channel_id=1, replica_groups={{17,19,21,23,25,27,29,31,1,3,5,7,9,11,13,15},{49,51,53,55,57,59,61,63,3..., dimensions={0} | all-to-all | bytes 524288 | tf_op jit(solution)/shard_map/all_to_all | solution.py:25
  63.1 1.8 %all-gather.2 = f32[4,8,256]{2,1,0:T(8,128)S(1)} all-gather(f32[2,8,256]{2,1,0:T(8,128)S(1)} %shard_map.49), channel_id=4, replica_groups=mesh['xh'=2,'y'=8,'xl'=2,'z'=16,'core'=2] {'core'}, dimensions={0}, use_global_device_ids=true | all-gather | bytes 49152 | tf_op jit(solution)/shard_map/all_gather | solution.py:123
  64.9 0.6 shard_map.50
  (4 shorter events, 0.0 us)
Async XLA Ops:
  15.8 15.2 %collective-permute-start = (bf16[32,128,128]{2,1,0:T(8,128)(2,1)}, bf16[32,128,128]{2,1,0:T(8,128)(2,1)S(1)}, u32[]{:S(2)}, u32[]{:S(2)}) collective-permute-start(bf16[32,128,128]{2,1,0:T(8,128)(2,1)} %tiles.1), channel_id=1, source_target_pairs={{0,1},{1,0},{2,3},{3,2},{4,5},{5,4},{6,7},{7,6},{8,9},{9,8},{10,11... | collective-permute-start | bytes 3145736 | tf_op jit(solution)/shard_map/ppermute | solution.py:109
  18.6 9.2 %copy-start.1 = (s32[32]{0:T(128)S(1)}, s32[32]{0:T(128)}, u32[]{:S(2)}) copy-start(s32[32]{0:T(128)} %param.7) | copy-start | bytes 388
  18.6 9.2 %copy-start.2 = (s32[32]{0:T(128)S(1)}, s32[32]{0:T(128)}, u32[]{:S(2)}) copy-start(s32[32]{0:T(128)} %param.6) | copy-start | bytes 388
  18.6 12.3 %all-to-all-start = ((bf16[16,2,8,256]{3,2,1,0:T(8,128)(2,1)}), bf16[16,2,8,256]{3,2,1,0:T(8,128)(2,1)S(1)}, u32[]{:S(2)}, u32[]{:S(2)}) async-start(bf16[16,2,8,256]{3,2,1,0:T(8,128)(2,1)} %broadcast_in_dim.2), calls=%async_computation | async-start | bytes 262144 | tf_op jit(solution)/shard_map/all_to_all | solution.py:25
  29.7 1.3 %copy-start = (bf16[32,128,128]{2,1,0:T(8,128)(2,1)S(1)}, bf16[32,128,128]{2,1,0:T(8,128)(2,1)}, u32[]{:S(2)}) copy-start(bf16[32,128,128]{2,1,0:T(8,128)(2,1)} %tiles.1) | copy-start | bytes 3145732
  32.8 7.1 %collective-permute-start.2 = (f32[64,8,128]{2,1,0:T(8,128)S(1)}, f32[64,8,128]{2,1,0:T(8,128)S(1)}, u32[]{:S(2)}, u32[]{:S(2)}) collective-permute-start(f32[64,8,128]{2,1,0:T(8,128)S(1)} %get-tuple-element.18), channel_id=1, source_target_pairs={{1,33},{3,35},{5,37},{7,39},{9,41},{11,43},{13,45},{15,47},{17,49}... | collective-permute-start | bytes 786440 | tf_op jit(solution)/shard_map/ppermute | solution.py:116
  34.9 0.7 %collective-permute-start.1 = (bf16[16,2,8,256]{3,2,1,0:T(8,128)(2,1)S(1)}, bf16[16,2,8,256]{3,2,1,0:T(8,128)(2,1)S(1)}, u32[]{:S(2)}, u32[]{:S(2)}) collective-permute-start(bf16[16,2,8,256]{3,2,1,0:T(8,128)(2,1)S(1)} %all-to-all-done.far), channel_id=1, source_target_pairs={{0,32},{2,34},{4,36},{6,38},{8,40},{10,42},{12,44},{14,46},{16,48}... | collective-permute-start | bytes 393224 | tf_op jit(solution)/shard_map/ppermute | solution.py:114

commit v5 on v4

--- a/solution.py
+++ b/solution.py
@@ -11,6 +11,7 @@
 TPD, K, TILE, SEG = 32, 8, 128, 256
 FIRST_Z = (12, 8)
 FIRST_ROW = 12
+LEVELS = 32000.0
 SWAP = [(0, 1), (1, 0)]
 VM = pl.BlockSpec(memory_space=pltpu.VMEM)
 SM = pl.BlockSpec(memory_space=pltpu.SMEM)
@@ -59,28 +60,45 @@
                 send[r & 63] += jnp.where(here, 0.0, y)
 
 
-def col_kernel(at, far, far_other, mine, other, tiles, tiles_other, out):
+def encode(sums, out):
+    for p in range(16):
+        blocks = [sums[4 * p + j] for j in range(4)]
+        top = [jnp.max(jnp.abs(x), axis=0, keepdims=True) for x in blocks]
+        top = jnp.concatenate(top + [jnp.zeros((4, TILE), F32)], axis=0)
+        e = jnp.ceil(jnp.log2(jnp.maximum(top, 2.0**-110)))
+        scale = jnp.exp2(-e) * LEVELS
+        for j, x in enumerate(blocks):
+            out[p, j] = jnp.round(x * scale[j : j + 1]).astype(jnp.int32).astype(jnp.int16)
+        out[p, 4] = e.astype(jnp.int32).astype(jnp.int16)
+
+
+def col_kernel(at, far, far_other, mine, other, tiles, tiles_other, out, acc):
     @pl.when(lax.axis_index("core") == 0)
     def _():
         xl = lax.axis_index("xl")
-        out[...] = jnp.zeros_like(out)
+        acc[...] = jnp.zeros_like(acc)
         for core, blocks in ((1, tiles_other), (0, tiles)):
             for t in range(TPD):
                 r, c = at[3 * core, t], at[3 * core + 2, t]
                 z, d = (r >> 2) & 15, (r >> 1) & 1
                 x = half_of(jnp.where((r >> 6) == xl, far[z, d], far_other[z, d]), r & 1)
-                out[(c >> 1) * 4 + 2 * core + (c & 1)] += jnp.dot(x, blocks[t], preferred_element_type=F32)
+                acc[(c >> 1) * 4 + 2 * core + (c & 1)] += jnp.dot(x, blocks[t], preferred_element_type=F32)
 
     @pl.when(lax.axis_index("core") == 1)
     def _():
-        out[...] = mine[...] + other[...]
+        acc[...] = mine[...] + other[...]
+
+    encode(acc, out)
 
 
 def sum_kernel(got, out):
-    s = jnp.sum(got[...], axis=0)
+    total = [jnp.zeros((K, TILE), F32)] * 4
+    for p in range(16):
+        unit = jnp.exp2(got[p, 4].astype(jnp.int32).astype(F32)) * (1.0 / LEVELS)
+        total = [x + got[p, j].astype(jnp.int32).astype(F32) * unit[j : j + 1] for j, x in enumerate(total)]
     for c in range(2):
-        out[c, :, :TILE] = s[2 * c]
-        out[c, :, TILE:] = s[2 * c + 1]
+        out[c, :, :TILE] = total[2 * c]
+        out[c, :, TILE:] = total[2 * c + 1]
 
 
 def total_kernel(both, out):
@@ -88,13 +106,14 @@
     out[...] = both[0, core] + both[1, core]
 
 
-def call(kernel, shapes, specs, *args, flops=0, dtype=F32):
+def call(kernel, shapes, specs, *args, flops=0, dtype=F32, scratch=()):
     outs = [jax.ShapeDtypeStruct(shape, dtype) for shape in shapes]
     return pl.pallas_call(
         kernel,
         out_shape=outs,
         in_specs=specs,
         out_specs=[VM] * len(outs),
+        scratch_shapes=scratch,
         cost_estimate=pl.CostEstimate(flops=flops, bytes_accessed=1 << 20, transcendentals=0),
         compiler_params=pltpu.CompilerParams(vmem_limit_bytes=16 << 20),
     )(*args)
@@ -115,10 +134,10 @@
     mine, send = call(row_kernel, [sums, sums], [SM, VM, VM, VM], at, far, tiles, tiles_other, flops=flops)
     other = lax.ppermute(send, AXES, between(1))
     (part,) = call(
-        col_kernel, [sums], [SM, VM, VM, VM, VM, VM, VM], at, far, far_other, mine, other, tiles, tiles_other,
-        flops=flops,
+        col_kernel, [(16, 5, K, TILE)], [SM, VM, VM, VM, VM, VM, VM], at, far, far_other, mine, other, tiles, tiles_other,
+        flops=flops, dtype=jnp.int16, scratch=[pltpu.VMEM(sums, F32)],
     )
-    got = exchange(part.reshape(16, 4, K, TILE), 1, FIRST_Z[1])
+    got = exchange(part, 1, FIRST_Z[1])
     (part,) = call(sum_kernel, [(2, K, SEG)], [VM], got)
     (out,) = call(total_kernel, [(K, SEG)], [VM], lax.all_gather(part, "core", axis=0))
     return out

time: 65.9 us -> 63.9 us (0.970)
  blocking collectives: 41.9 us -> 39.8 us
    all_to_all x1, blocking collectives: 22.5 us -> 20.4 us  [exchange(): return lax.all_to_all(x, AXES, 0, 0, axis_index_groups=groups, tiled=True)]
where the time goes in v5:
time: 63.9 us; the launch traced here: 63.6 us
  blocking collectives  39.8 us (62%)
  starting transfers between devices  14.2 us (22%)
  waiting for transfers between devices  5.63 us (9%)
  Pallas kernels  3.26 us (5%)
  local copies, waits for them, and re-layouts  0.67 us (1%)
    all_to_all x1, blocking collectives, exchange(): return lax.all_to_all(x, AXES, 0, 0, axis_index_groups=groups, tiled=True)  20.4 us
    all_gather x1, blocking collectives, per_device(): both = lax.all_gather(v, 'core', axis=0)  15.8 us
    all_to_all x1, starting transfers between devices, exchange(): return lax.all_to_all(x, AXES, 0, 0, axis_index_groups=groups, tiled=True)  9.2 us
    ppermute x1, waiting for transfers between devices, per_device(): other = lax.ppermute(send, AXES, between(1))  4.34 us
    pallas_call x5, Pallas kernels, call(): pl.pallas_call(kernel, out_shape=outs, in_specs=specs, out_specs=[VM] * l...  3.26 us
    ppermute x1, starting transfers between devices, per_device(): tiles_other = lax.ppermute(tiles, 'core', SWAP)  2.2 us
    ppermute x1, starting transfers between devices, per_device(): other = lax.ppermute(send, AXES, between(1))  2.08 us
    all_gather x1, blocking collectives, per_device(): lax.all_gather(part, 'core', axis=0)  1.83 us
  transfers between devices with their start and end apart: 4, of which 2 were waited for; matrix products, arithmetic and copies ran while one was open for 1% of the time, Pallas kernels for 0%

profile of v5, /device:TPU:1, one launch (start us, length us, event | category | flops | bytes accessed | tf_op | source)
XLA Modules:
  0.0 63.6 jit_solution(4097217067904928310)
XLA Ops:
  0.0 15.8 %all-gather = bf16[16,256]{1,0:T(8,128)(2,1)S(1)} all-gather(bf16[8,256]{1,0:T(8,128)(2,1)} %param.4), channel_id=2, replica_groups=mesh['xh'=2,'y'=8,'xl'=2,'z'=16,'core'=2] {'core'}, dimensions={0}, use_global_device_ids=true | all-gather | bytes 12288 | tf_op jit(solution)/shard_map/all_gather | solution.py:125
  15.8 2.2 %collective-permute-start = (bf16[32,128,128]{2,1,0:T(8,128)(2,1)}, bf16[32,128,128]{2,1,0:T(8,128)(2,1)S(1)}, u32[]{:S(2)}, u32[]{:S(2)}) collective-permute-start(bf16[32,128,128]{2,1,0:T(8,128)(2,1)} %tiles.1), channel_id=1, source_target_pairs={{0,1},{1,0},{2,3},{3,2},{4,5},{5,4},{6,7},{7,6},{8,9},{9,8},{10,11... | collective-permute-start | bytes 3145736 | tf_op jit(solution)/shard_map/ppermute | solution.py:128
  18.0 0.7 %broadcast_in_dim.2 = bf16[16,2,8,256]{3,2,1,0:T(8,128)(2,1)} broadcast(bf16[2,8,256]{2,1,0:T(8,128)(2,1)S(1)} %bitcast.9), dimensions={1,2,3} | broadcast | bytes 139264 | tf_op jit(solution)/shard_map/broadcast_in_dim | solution.py:127
  18.6 0.0 copy-start.1
  18.6 0.0 copy-start.2
  18.6 9.2 %all-to-all-start = ((bf16[16,2,8,256]{3,2,1,0:T(8,128)(2,1)}), bf16[16,2,8,256]{3,2,1,0:T(8,128)(2,1)S(1)}, u32[]{:S(2)}, u32[]{:S(2)}) async-start(bf16[16,2,8,256]{3,2,1,0:T(8,128)(2,1)} %broadcast_in_dim.2), calls=%async_computation | async-start | bytes 262144 | tf_op jit(solution)/shard_map/all_to_all | solution.py:26
  27.8 0.0 copy-done.1
  27.8 0.0 copy-done.2
  27.9 1.8 %all-gather.1 = bf16[16,128]{1,0:T(8,128)(2,1)S(1)} all-gather(bf16[8,128]{1,0:T(8,128)(2,1)S(1)} %fusion.5), channel_id=3, replica_groups=mesh['xh'=2,'y'=8,'xl'=2,'z'=16,'core'=2] {'core'}, dimensions={0}, use_global_device_ids=true | all-gather | bytes 6144 | tf_op jit(solution)/shard_map/all_gather | solution.py:130
  29.7 0.0 copy-start
  29.7 1.3 %all-to-all-done.far = bf16[16,2,8,256]{3,2,1,0:T(8,128)(2,1)S(1)} async-done(((bf16[16,2,8,256]{3,2,1,0:T(8,128)(2,1)}), bf16[16,2,8,256]{3,2,1,0:T(8,128)(2,1)S(1)}, u32[]{:S(2)}, u32[]{:S(2)}) %all-to-all-start) | async-done | bytes 131104 | tf_op jit(solution)/shard_map/all_to_all | solution.py:26
  31.0 0.0 collective-permute-done.tiles_other
  31.0 0.0 copy-done
  31.0 1.8 %shard_map.47 = (f32[64,8,128]{2,1,0:T(8,128)S(1)}, f32[64,8,128]{2,1,0:T(8,128)S(1)}) custom-call(s32[8,128]{1,0:T(8,128)S(1)} %shard_map.46.at, bf16[16,2,8,256]{3,2,1,0:T(8,128)(2,1)S(1)} %all-to-all-done.far, bf16[32,128,128]{2,1,0:T(8,128)(2,1)S(1)} %copy-done, bf16[32,128,128]{2,1,0:T(8,128)(2,1)S(1)} %collective-permute-done.tiles_other), custom_call_target="tpu_custom_call" | custom-call | flops 16777216 | bytes 1048576 | tf_op jit(solution)/shard_map/pallas_call | solution.py:111
  32.8 2.1 %collective-permute-start.2 = (f32[64,8,128]{2,1,0:T(8,128)S(1)}, f32[64,8,128]{2,1,0:T(8,128)S(1)}, u32[]{:S(2)}, u32[]{:S(2)}) collective-permute-start(f32[64,8,128]{2,1,0:T(8,128)S(1)} %get-tuple-element.18), channel_id=1, source_target_pairs={{1,33},{3,35},{5,37},{7,39},{9,41},{11,43},{13,45},{15,47},{17,49}... | collective-permute-start | bytes 786440 | tf_op jit(solution)/shard_map/ppermute | solution.py:135
  34.9 0.7 %collective-permute-start.1 = (bf16[16,2,8,256]{3,2,1,0:T(8,128)(2,1)S(1)}, bf16[16,2,8,256]{3,2,1,0:T(8,128)(2,1)S(1)}, u32[]{:S(2)}, u32[]{:S(2)}) collective-permute-start(bf16[16,2,8,256]{3,2,1,0:T(8,128)(2,1)S(1)} %all-to-all-done.far), channel_id=1, source_target_pairs={{0,32},{2,34},{4,36},{6,38},{8,40},{10,42},{12,44},{14,46},{16,48}... | collective-permute-start | bytes 393224 | tf_op jit(solution)/shard_map/ppermute | solution.py:133
  35.6 0.0 collective-permute-done.1.far_other
  35.6 4.3 %collective-permute-done.2.other = f32[64,8,128]{2,1,0:T(8,128)S(1)} collective-permute-done((f32[64,8,128]{2,1,0:T(8,128)S(1)}, f32[64,8,128]{2,1,0:T(8,128)S(1)}, u32[]{:S(2)}, u32[]{:S(2)}) %collective-permute-start.2) | collective-permute-done | bytes 262176 | tf_op jit(solution)/shard_map/ppermute | solution.py:135
  39.9 0.8 %shard_map.48 = s16[16,5,8,128]{3,2,1,0:T(8,128)(2,1)S(1)} custom-call(s32[8,128]{1,0:T(8,128)S(1)} %shard_map.46.at, bf16[16,2,8,256]{3,2,1,0:T(8,128)(2,1)S(1)} %all-to-all-done.far, bf16[16,2,8,256]{3,2,1,0:T(8,128)(2,1)S(1)} %collective-permute-done.1.far_other, f32[64,8,128]{2,1,0:T(8,128)S(1)} %get-tuple-element.17.mine, ...), custom_call_target="tpu_custom_call" | custom-call | flops 16777216 | bytes 1048576 | tf_op jit(solution)/shard_map/pallas_call | solution.py:111
  40.7 20.4 %all_to_all.10.got = s16[16,5,8,128]{3,2,1,0:T(8,128)(2,1)S(1)} all-to-all(s16[16,5,8,128]{3,2,1,0:T(8,128)(2,1)S(1)} %shard_map.48), channel_id=1, replica_groups={{17,19,21,23,25,27,29,31,1,3,5,7,9,11,13,15},{49,51,53,55,57,59,61,63,3..., dimensions={0} | all-to-all | bytes 327680 | tf_op jit(solution)/shard_map/all_to_all | solution.py:26
  61.1 0.1 shard_map.49
  61.2 1.8 %all-gather.2 = f32[4,8,256]{2,1,0:T(8,128)S(1)} all-gather(f32[2,8,256]{2,1,0:T(8,128)S(1)} %shard_map.49), channel_id=4, replica_groups=mesh['xh'=2,'y'=8,'xl'=2,'z'=16,'core'=2] {'core'}, dimensions={0}, use_global_device_ids=true | all-gather | bytes 49152 | tf_op jit(solution)/shard_map/all_gather | solution.py:142
  63.0 0.6 shard_map.50
  (3 shorter events, 0.0 us)
Async XLA Ops:
  15.8 15.2 %collective-permute-start = (bf16[32,128,128]{2,1,0:T(8,128)(2,1)}, bf16[32,128,128]{2,1,0:T(8,128)(2,1)S(1)}, u32[]{:S(2)}, u32[]{:S(2)}) collective-permute-start(bf16[32,128,128]{2,1,0:T(8,128)(2,1)} %tiles.1), channel_id=1, source_target_pairs={{0,1},{1,0},{2,3},{3,2},{4,5},{5,4},{6,7},{7,6},{8,9},{9,8},{10,11... | collective-permute-start | bytes 3145736 | tf_op jit(solution)/shard_map/ppermute | solution.py:128
  18.6 9.2 %copy-start.1 = (s32[32]{0:T(128)S(1)}, s32[32]{0:T(128)}, u32[]{:S(2)}) copy-start(s32[32]{0:T(128)} %param.7) | copy-start | bytes 388
  18.6 9.2 %copy-start.2 = (s32[32]{0:T(128)S(1)}, s32[32]{0:T(128)}, u32[]{:S(2)}) copy-start(s32[32]{0:T(128)} %param.6) | copy-start | bytes 388
  18.6 12.3 %all-to-all-start = ((bf16[16,2,8,256]{3,2,1,0:T(8,128)(2,1)}), bf16[16,2,8,256]{3,2,1,0:T(8,128)(2,1)S(1)}, u32[]{:S(2)}, u32[]{:S(2)}) async-start(bf16[16,2,8,256]{3,2,1,0:T(8,128)(2,1)} %broadcast_in_dim.2), calls=%async_computation | async-start | bytes 262144 | tf_op jit(solution)/shard_map/all_to_all | solution.py:26
  29.7 1.3 %copy-start = (bf16[32,128,128]{2,1,0:T(8,128)(2,1)S(1)}, bf16[32,128,128]{2,1,0:T(8,128)(2,1)}, u32[]{:S(2)}) copy-start(bf16[32,128,128]{2,1,0:T(8,128)(2,1)} %tiles.1) | copy-start | bytes 3145732
  32.8 7.1 %collective-permute-start.2 = (f32[64,8,128]{2,1,0:T(8,128)S(1)}, f32[64,8,128]{2,1,0:T(8,128)S(1)}, u32[]{:S(2)}, u32[]{:S(2)}) collective-permute-start(f32[64,8,128]{2,1,0:T(8,128)S(1)} %get-tuple-element.18), channel_id=1, source_target_pairs={{1,33},{3,35},{5,37},{7,39},{9,41},{11,43},{13,45},{15,47},{17,49}... | collective-permute-start | bytes 786440 | tf_op jit(solution)/shard_map/ppermute | solution.py:135
  34.9 0.7 %collective-permute-start.1 = (bf16[16,2,8,256]{3,2,1,0:T(8,128)(2,1)S(1)}, bf16[16,2,8,256]{3,2,1,0:T(8,128)(2,1)S(1)}, u32[]{:S(2)}, u32[]{:S(2)}) collective-permute-start(bf16[16,2,8,256]{3,2,1,0:T(8,128)(2,1)S(1)} %all-to-all-done.far), channel_id=1, source_target_pairs={{0,32},{2,34},{4,36},{6,38},{8,40},{10,42},{12,44},{14,46},{16,48}... | collective-permute-start | bytes 393224 | tf_op jit(solution)/shard_map/ppermute | solution.py:133

commit v6 on v5

--- a/solution.py
+++ b/solution.py
@@ -44,7 +44,7 @@
         out[3 * core + 2 : 3 * core + 3, :] = (c - 2 * FIRST_ROW) & 31
 
 
-def row_kernel(at, far, tiles, tiles_other, mine, send):
+def row_kernel(at, far, tiles, tiles_other, mine, out, send):
     @pl.when(lax.axis_index("core") == 1)
     def _():
         xl = lax.axis_index("xl")
@@ -58,6 +58,15 @@
                 here = (r >> 6) == xl
                 mine[r & 63] += jnp.where(here, y, 0.0)
                 send[r & 63] += jnp.where(here, 0.0, y)
+        encode(send, out)
+
+
+def unit_of(coded, p):
+    return jnp.exp2(coded[p, 4].astype(jnp.int32).astype(F32)) * (1.0 / LEVELS)
+
+
+def value_of(coded, p, j, unit):
+    return coded[p, j].astype(jnp.int32).astype(F32) * unit[j : j + 1]
 
 
 def encode(sums, out):
@@ -86,7 +95,10 @@
 
     @pl.when(lax.axis_index("core") == 1)
     def _():
-        acc[...] = mine[...] + other[...]
+        for p in range(16):
+            unit = unit_of(other, p)
+            for j in range(4):
+                acc[4 * p + j] = mine[4 * p + j] + value_of(other, p, j, unit)
 
     encode(acc, out)
 
@@ -94,8 +106,8 @@
 def sum_kernel(got, out):
     total = [jnp.zeros((K, TILE), F32)] * 4
     for p in range(16):
-        unit = jnp.exp2(got[p, 4].astype(jnp.int32).astype(F32)) * (1.0 / LEVELS)
-        total = [x + got[p, j].astype(jnp.int32).astype(F32) * unit[j : j + 1] for j, x in enumerate(total)]
+        unit = unit_of(got, p)
+        total = [x + value_of(got, p, j, unit) for j, x in enumerate(total)]
     for c in range(2):
         out[c, :, :TILE] = total[2 * c]
         out[c, :, TILE:] = total[2 * c + 1]
@@ -106,11 +118,10 @@
     out[...] = both[0, core] + both[1, core]
 
 
-def call(kernel, shapes, specs, *args, flops=0, dtype=F32, scratch=()):
-    outs = [jax.ShapeDtypeStruct(shape, dtype) for shape in shapes]
+def call(kernel, outs, specs, *args, flops=0, scratch=()):
     return pl.pallas_call(
         kernel,
-        out_shape=outs,
+        out_shape=[jax.ShapeDtypeStruct(*out) for out in outs],
         in_specs=specs,
         out_specs=[VM] * len(outs),
         scratch_shapes=scratch,
@@ -121,25 +132,28 @@
 
 def per_device(v, tiles, tr, tc):
     flops = 4 * TPD * K * TILE * TILE
-    sums = (64, K, TILE)
+    sums, coded = (64, K, TILE), ((16, 5, K, TILE), jnp.int16)
     both = lax.all_gather(v, "core", axis=0)
     both, tiles = lax.optimization_barrier((both, tiles))
     far = exchange(jnp.broadcast_to(both[None], (16, 2, K, SEG)), 0, FIRST_Z[0])
     tiles_other = lax.ppermute(tiles, "core", SWAP)
     places = jnp.pad(jnp.stack([tr, tc]).astype(v.dtype), ((0, K - 2), (0, TILE - TPD)))
     places = lax.all_gather(places, "core", axis=0)
-    (at,) = call(place_kernel, [(8, TILE)], [VM], places, dtype=jnp.int32, flops=7000000000)
+    (at,) = call(place_kernel, [((8, TILE), jnp.int32)], [VM], places, flops=7000000000)
     far, at, tiles_other = lax.optimization_barrier((far, at, tiles_other))
     far_other = lax.ppermute(far, AXES, between(0))
-    mine, send = call(row_kernel, [sums, sums], [SM, VM, VM, VM], at, far, tiles, tiles_other, flops=flops)
+    scratch = [pltpu.VMEM(sums, F32)]
+    mine, send = call(
+        row_kernel, [(sums, F32), coded], [SM, VM, VM, VM], at, far, tiles, tiles_other, flops=flops, scratch=scratch
+    )
     other = lax.ppermute(send, AXES, between(1))
     (part,) = call(
-        col_kernel, [(16, 5, K, TILE)], [SM, VM, VM, VM, VM, VM, VM], at, far, far_other, mine, other, tiles, tiles_other,
-        flops=flops, dtype=jnp.int16, scratch=[pltpu.VMEM(sums, F32)],
+        col_kernel, [coded], [SM, VM, VM, VM, VM, VM, VM], at, far, far_other, mine, other, tiles, tiles_other,
+        flops=flops, scratch=scratch,
     )
     got = exchange(part, 1, FIRST_Z[1])
-    (part,) = call(sum_kernel, [(2, K, SEG)], [VM], got)
-    (out,) = call(total_kernel, [(K, SEG)], [VM], lax.all_gather(part, "core", axis=0))
+    (part,) = call(sum_kernel, [((2, K, SEG), F32)], [VM], got)
+    (out,) = call(total_kernel, [((K, SEG), F32)], [VM], lax.all_gather(part, "core", axis=0))
     return out
 
 

time: 63.9 us -> 63.5 us (level)
  waiting for transfers between devices: 5.63 us -> 4.58 us
    all_gather x1, blocking collectives: 1.83 us -> 2.98 us  [per_device(): lax.all_gather(part, 'core', axis=0)]
    ppermute x1, waiting for transfers between devices: 4.34 us -> 3.28 us  [per_device(): other = lax.ppermute(send, AXES, between(1))]
    all_to_all x1, blocking collectives: 20.4 us -> 19.8 us  [exchange(): return lax.all_to_all(x, AXES, 0, 0, axis_index_groups=groups, tiled=True)]
where the time goes in v6:
time: 63.5 us; the launch traced here: 63.2 us
  blocking collectives  40.3 us (63%)
  starting transfers between devices  14.2 us (22%)
  waiting for transfers between devices  4.58 us (7%)
  Pallas kernels  3.43 us (5%)
  local copies, waits for them, and re-layouts  0.67 us (1%)
    all_to_all x1, blocking collectives, exchange(): return lax.all_to_all(x, AXES, 0, 0, axis_index_groups=groups, tiled=True)  19.8 us
    all_gather x1, blocking collectives, per_device(): both = lax.all_gather(v, 'core', axis=0)  15.8 us
    all_to_all x1, starting transfers between devices, exchange(): return lax.all_to_all(x, AXES, 0, 0, axis_index_groups=groups, tiled=True)  9.2 us
    pallas_call x5, Pallas kernels, call(): pl.pallas_call(kernel, out_shape=[jax.ShapeDtypeStruct(*out) for out in o...  3.43 us
    ppermute x1, waiting for transfers between devices, per_device(): other = lax.ppermute(send, AXES, between(1))  3.28 us
    all_gather x1, blocking collectives, per_device(): lax.all_gather(part, 'core', axis=0)  2.98 us
    ppermute x1, starting transfers between devices, per_device(): tiles_other = lax.ppermute(tiles, 'core', SWAP)  2.2 us
    ppermute x1, starting transfers between devices, per_device(): other = lax.ppermute(send, AXES, between(1))  2.09 us
  transfers between devices with their start and end apart: 4, of which 2 were waited for; matrix products, arithmetic and copies ran while one was open for 1% of the time, Pallas kernels for 0%

profile of v6, /device:TPU:1, one launch (start us, length us, event | category | flops | bytes accessed | tf_op | source)
XLA Modules:
  0.0 63.2 jit_solution(14604345821075980398)
XLA Ops:
  0.0 15.8 %all-gather = bf16[16,256]{1,0:T(8,128)(2,1)S(1)} all-gather(bf16[8,256]{1,0:T(8,128)(2,1)} %param.4), channel_id=2, replica_groups=mesh['xh'=2,'y'=8,'xl'=2,'z'=16,'core'=2] {'core'}, dimensions={0}, use_global_device_ids=true | all-gather | bytes 12288 | tf_op jit(solution)/shard_map/all_gather | solution.py:136
  15.8 2.2 %collective-permute-start = (bf16[32,128,128]{2,1,0:T(8,128)(2,1)}, bf16[32,128,128]{2,1,0:T(8,128)(2,1)S(1)}, u32[]{:S(2)}, u32[]{:S(2)}) collective-permute-start(bf16[32,128,128]{2,1,0:T(8,128)(2,1)} %tiles.1), channel_id=1, source_target_pairs={{0,1},{1,0},{2,3},{3,2},{4,5},{5,4},{6,7},{7,6},{8,9},{9,8},{10,11... | collective-permute-start | bytes 3145736 | tf_op jit(solution)/shard_map/ppermute | solution.py:139
  18.0 0.7 %broadcast_in_dim.2 = bf16[16,2,8,256]{3,2,1,0:T(8,128)(2,1)} broadcast(bf16[2,8,256]{2,1,0:T(8,128)(2,1)S(1)} %bitcast.9), dimensions={1,2,3} | broadcast | bytes 139264 | tf_op jit(solution)/shard_map/broadcast_in_dim | solution.py:138
  18.6 0.0 copy-start.1
  18.6 0.0 copy-start.2
  18.6 9.2 %all-to-all-start = ((bf16[16,2,8,256]{3,2,1,0:T(8,128)(2,1)}), bf16[16,2,8,256]{3,2,1,0:T(8,128)(2,1)S(1)}, u32[]{:S(2)}, u32[]{:S(2)}) async-start(bf16[16,2,8,256]{3,2,1,0:T(8,128)(2,1)} %broadcast_in_dim.2), calls=%async_computation | async-start | bytes 262144 | tf_op jit(solution)/shard_map/all_to_all | solution.py:26
  27.8 0.0 copy-done.1
  27.8 0.0 copy-done.2
  27.9 1.8 %all-gather.1 = bf16[16,128]{1,0:T(8,128)(2,1)S(1)} all-gather(bf16[8,128]{1,0:T(8,128)(2,1)S(1)} %fusion.5), channel_id=3, replica_groups=mesh['xh'=2,'y'=8,'xl'=2,'z'=16,'core'=2] {'core'}, dimensions={0}, use_global_device_ids=true | all-gather | bytes 6144 | tf_op jit(solution)/shard_map/all_gather | solution.py:141
  29.7 0.0 copy-start
  29.7 1.3 %all-to-all-done.far = bf16[16,2,8,256]{3,2,1,0:T(8,128)(2,1)S(1)} async-done(((bf16[16,2,8,256]{3,2,1,0:T(8,128)(2,1)}), bf16[16,2,8,256]{3,2,1,0:T(8,128)(2,1)S(1)}, u32[]{:S(2)}, u32[]{:S(2)}) %all-to-all-start) | async-done | bytes 131104 | tf_op jit(solution)/shard_map/all_to_all | solution.py:26
  31.0 0.0 collective-permute-done.tiles_other
  31.0 0.0 copy-done
  31.0 2.0 %shard_map.47 = (f32[64,8,128]{2,1,0:T(8,128)S(1)}, s16[16,5,8,128]{3,2,1,0:T(8,128)(2,1)S(1)}) custom-call(s32[8,128]{1,0:T(8,128)S(1)} %shard_map.46.at, bf16[16,2,8,256]{3,2,1,0:T(8,128)(2,1)S(1)} %all-to-all-done.far, bf16[32,128,128]{2,1,0:T(8,128)(2,1)S(1)} %copy-done, bf16[32,128,128]{2,1,0:T(8,128)(2,1)S(1)} %collective-permute-done.tiles_other), custom_call_target="tpu_custom_call" | custom-call | flops 16777216 | bytes 1048576 | tf_op jit(solution)/shard_map/pallas_call | solution.py:122
  32.9 2.1 %collective-permute-start.2 = (s16[16,5,8,128]{3,2,1,0:T(8,128)(2,1)S(1)}, s16[16,5,8,128]{3,2,1,0:T(8,128)(2,1)S(1)}, u32[]{:S(2)}, u32[]{:S(2)}) collective-permute-start(s16[16,5,8,128]{3,2,1,0:T(8,128)(2,1)S(1)} %get-tuple-element.18), channel_id=1, source_target_pairs={{1,33},{3,35},{5,37},{7,39},{9,41},{11,43},{13,45},{15,47},{17,49}... | collective-permute-start | bytes 491528 | tf_op jit(solution)/shard_map/ppermute | solution.py:149
  35.0 0.7 %collective-permute-start.1 = (bf16[16,2,8,256]{3,2,1,0:T(8,128)(2,1)S(1)}, bf16[16,2,8,256]{3,2,1,0:T(8,128)(2,1)S(1)}, u32[]{:S(2)}, u32[]{:S(2)}) collective-permute-start(bf16[16,2,8,256]{3,2,1,0:T(8,128)(2,1)S(1)} %all-to-all-done.far), channel_id=1, source_target_pairs={{0,32},{2,34},{4,36},{6,38},{8,40},{10,42},{12,44},{14,46},{16,48}... | collective-permute-start | bytes 393224 | tf_op jit(solution)/shard_map/ppermute | solution.py:144
  35.7 0.0 collective-permute-done.1.far_other
  35.7 3.3 %collective-permute-done.2.other = s16[16,5,8,128]{3,2,1,0:T(8,128)(2,1)S(1)} collective-permute-done((s16[16,5,8,128]{3,2,1,0:T(8,128)(2,1)S(1)}, s16[16,5,8,128]{3,2,1,0:T(8,128)(2,1)S(1)}, u32[]{:S(2)}, u32[]{:S(2)}) %collective-permute-start.2) | collective-permute-done | bytes 163872 | tf_op jit(solution)/shard_map/ppermute | solution.py:149
  39.0 0.8 %shard_map.48 = s16[16,5,8,128]{3,2,1,0:T(8,128)(2,1)S(1)} custom-call(s32[8,128]{1,0:T(8,128)S(1)} %shard_map.46.at, bf16[16,2,8,256]{3,2,1,0:T(8,128)(2,1)S(1)} %all-to-all-done.far, bf16[16,2,8,256]{3,2,1,0:T(8,128)(2,1)S(1)} %collective-permute-done.1.far_other, f32[64,8,128]{2,1,0:T(8,128)S(1)} %get-tuple-element.17.mine, ...), custom_call_target="tpu_custom_call" | custom-call | flops 16777216 | bytes 1048576 | tf_op jit(solution)/shard_map/pallas_call | solution.py:122
  39.8 19.8 %all_to_all.10.got = s16[16,5,8,128]{3,2,1,0:T(8,128)(2,1)S(1)} all-to-all(s16[16,5,8,128]{3,2,1,0:T(8,128)(2,1)S(1)} %shard_map.48), channel_id=1, replica_groups={{17,19,21,23,25,27,29,31,1,3,5,7,9,11,13,15},{49,51,53,55,57,59,61,63,3..., dimensions={0} | all-to-all | bytes 327680 | tf_op jit(solution)/shard_map/all_to_all | solution.py:26
  59.6 0.1 shard_map.49
  59.6 3.0 %all-gather.2 = f32[4,8,256]{2,1,0:T(8,128)S(1)} all-gather(f32[2,8,256]{2,1,0:T(8,128)S(1)} %shard_map.49), channel_id=4, replica_groups=mesh['xh'=2,'y'=8,'xl'=2,'z'=16,'core'=2] {'core'}, dimensions={0}, use_global_device_ids=true | all-gather | bytes 49152 | tf_op jit(solution)/shard_map/all_gather | solution.py:156
  62.6 0.6 shard_map.50
  (3 shorter events, 0.0 us)
Async XLA Ops:
  15.8 15.2 %collective-permute-start = (bf16[32,128,128]{2,1,0:T(8,128)(2,1)}, bf16[32,128,128]{2,1,0:T(8,128)(2,1)S(1)}, u32[]{:S(2)}, u32[]{:S(2)}) collective-permute-start(bf16[32,128,128]{2,1,0:T(8,128)(2,1)} %tiles.1), channel_id=1, source_target_pairs={{0,1},{1,0},{2,3},{3,2},{4,5},{5,4},{6,7},{7,6},{8,9},{9,8},{10,11... | collective-permute-start | bytes 3145736 | tf_op jit(solution)/shard_map/ppermute | solution.py:139
  18.6 9.2 %copy-start.1 = (s32[32]{0:T(128)S(1)}, s32[32]{0:T(128)}, u32[]{:S(2)}) copy-start(s32[32]{0:T(128)} %param.7) | copy-start | bytes 388
  18.6 9.2 %copy-start.2 = (s32[32]{0:T(128)S(1)}, s32[32]{0:T(128)}, u32[]{:S(2)}) copy-start(s32[32]{0:T(128)} %param.6) | copy-start | bytes 388
  18.6 12.3 %all-to-all-start = ((bf16[16,2,8,256]{3,2,1,0:T(8,128)(2,1)}), bf16[16,2,8,256]{3,2,1,0:T(8,128)(2,1)S(1)}, u32[]{:S(2)}, u32[]{:S(2)}) async-start(bf16[16,2,8,256]{3,2,1,0:T(8,128)(2,1)} %broadcast_in_dim.2), calls=%async_computation | async-start | bytes 262144 | tf_op jit(solution)/shard_map/all_to_all | solution.py:26
  29.7 1.3 %copy-start = (bf16[32,128,128]{2,1,0:T(8,128)(2,1)S(1)}, bf16[32,128,128]{2,1,0:T(8,128)(2,1)}, u32[]{:S(2)}) copy-start(bf16[32,128,128]{2,1,0:T(8,128)(2,1)} %tiles.1) | copy-start | bytes 3145732
  32.9 6.1 %collective-permute-start.2 = (s16[16,5,8,128]{3,2,1,0:T(8,128)(2,1)S(1)}, s16[16,5,8,128]{3,2,1,0:T(8,128)(2,1)S(1)}, u32[]{:S(2)}, u32[]{:S(2)}) collective-permute-start(s16[16,5,8,128]{3,2,1,0:T(8,128)(2,1)S(1)} %get-tuple-element.18), channel_id=1, source_target_pairs={{1,33},{3,35},{5,37},{7,39},{9,41},{11,43},{13,45},{15,47},{17,49}... | collective-permute-start | bytes 491528 | tf_op jit(solution)/shard_map/ppermute | solution.py:149
  35.0 0.7 %collective-permute-start.1 = (bf16[16,2,8,256]{3,2,1,0:T(8,128)(2,1)S(1)}, bf16[16,2,8,256]{3,2,1,0:T(8,128)(2,1)S(1)}, u32[]{:S(2)}, u32[]{:S(2)}) collective-permute-start(bf16[16,2,8,256]{3,2,1,0:T(8,128)(2,1)S(1)} %all-to-all-done.far), channel_id=1, source_target_pairs={{0,32},{2,34},{4,36},{6,38},{8,40},{10,42},{12,44},{14,46},{16,48}... | collective-permute-start | bytes 393224 | tf_op jit(solution)/shard_map/ppermute | solution.py:144
